TPU v7x, 32 devices: a whole 2x2x4 slice. The times are simulated.
32 devices in a mesh: ctx: 8 (over y, x, core), tp: 4 (over z).
Axes of the slice: x: 2, y: 2, z: 4, core: 2. Of those that a mesh axis runs over, the one named last changes fastest.
Arguments:
- tokens_in: bfloat16 [4096, 2560], P('ctx'), may hold values from -1.5 to 1.5
- w_qa: bfloat16 [2560, 768], replicated, may hold values from -0.125 to 0.125
- w_kva: bfloat16 [2560, 288], replicated, may hold values from -0.125 to 0.125
- w_qb: bfloat16 [768, 3840], P(None, 'tp'), may hold values from -0.4375 to 0.4375
- w_kvb: bfloat16 [256, 5120], P(None, 'tp'), may hold values from -0.375 to 0.375
- w_out: bfloat16 [2560, 2560], P(None, 'tp'), may hold values from -1 to 1
- w_gate: bfloat16 [2560, 6400], P(None, 'tp'), may hold values from -0.125 to 0.125
- w_up: bfloat16 [2560, 6400], P(None, 'tp'), may hold values from -0.125 to 0.125
- w_down: bfloat16 [2560, 6400], P(None, 'tp'), may hold values from -0.15625 to 0.15625
- gain_in: float32 [2560], replicated, may hold values from 0.5 to 1.5
- gain_q: float32 [768], replicated, may hold values from 0.5 to 1.5
- gain_kv: float32 [256], replicated, may hold values from 0.5 to 1.5
- gain_mid: float32 [2560], replicated, may hold values from 0.5 to 1.5
- cotangent: bfloat16 [4096, 2560], P('ctx'), may hold values from -6 to 6
- block_map: int32 [8, 2], replicated, may hold values from 0 to 15, as said below
- doc_lengths: int32 [4], replicated, may hold values from 1 to 3072, as said below
Outputs:
- out: bfloat16 [4096, 2560], P('ctx')
- grad_in: float32 [4096, 2560], P('ctx')
- grad_w_qa: float32 [2560, 768], P('ctx')
- grad_w_kva: float32 [2560, 288], P('ctx')
- grad_w_qb: float32 [768, 3840], P('ctx', 'tp')
- grad_w_kvb: float32 [256, 5120], P('ctx', 'tp')
- grad_w_out: float32 [2560, 2560], P('ctx', 'tp')
- grad_w_gate: float32 [2560, 6400], P('ctx', 'tp')
- grad_w_up: float32 [2560, 6400], P('ctx', 'tp')
- grad_w_down: float32 [2560, 6400], P('ctx', 'tp')
- grad_gain_in: float32 [2560], P('ctx')
- grad_gain_q: float32 [768], P('ctx')
- grad_gain_kv: float32 [256], P('ctx')
- grad_gain_mid: float32 [2560], P('ctx')
Inputs may be any that keep to these rules, and one draw needn't show every extreme that they name: `block_map`: row c lists the two blocks of 256 context places whose tokens ctx index c holds, first the one in column 0, then the one in column 1. Column 0 holds each block of the first half of the context once, column 1 each block of the second half once. `doc_lengths`: the lengths sum to 4096. The first or the last sequence has 3072 tokens.
All inputs are finite; a program needn't handle non-finite values.
Results may differ from a plain program's by a relative error of at most 0.025.
Values may be sent and summed in bfloat16 or wider, within the bound.
A program may use at most 320 MiB of HBM per device.

v0:
```python
import functools
import math

import jax
import jax.numpy as jnp
import numpy as np
from jax import lax
from jax.experimental import pallas as pl
from jax.experimental.pallas import tpu as pltpu
from jax.sharding import PartitionSpec as P

KVR = 256
NOPE = 64
ROPE = 32
VDIM = 64
HEAD = NOPE + VDIM
WIDE = 2 * HEAD
MASKED = -1e30
SCORE_SCALE = (NOPE + ROPE) ** (-0.5)
EXP2_SCALE = SCORE_SCALE * math.log2(math.e)
FOLD_AT = 96
SUM_ROWS = 16
VMEM_LIMIT = 56 * 1024 * 1024

EPSILON = 1e-05
ROPE_BASE = 10000.0
RESIDUAL_SCALE = 1.4 / math.sqrt(62.0)


def dot_nn(left_op, right_op):
    return jnp.dot(left_op, right_op, preferred_element_type=jnp.float32)


def dot_nt(left_op, right_op):
    return lax.dot_general(
        left_op, right_op, (((1,), (1,)), ((), ())), preferred_element_type=jnp.float32
    )


def starts_of(lengths):
    starts = [jnp.int32(0)]
    for s in range(lengths.shape[0] - 1):
        starts.append(starts[-1] + lengths[s])
    return starts


def begin_of(place, starts):
    begin = jnp.zeros_like(place)
    for start in starts:
        begin = jnp.where(start <= place, start, begin)
    return begin


def pair_kind(key_block, query_block, starts, block_rows):
    key_first = key_block * block_rows
    query_first = query_block * block_rows
    early = begin_of(query_first, starts)
    late = begin_of(query_first + block_rows - 1, starts)
    needed = (key_block <= query_block) & (key_first + block_rows - 1 >= early)
    whole = (key_block < query_block) & (late <= key_first)
    return needed, whole


def mask_bias(key_block, query_block, starts, block_rows, keys_first):
    key_dim = 0 if keys_first else 1
    shape = (block_rows, block_rows)
    key_place = key_block * block_rows + lax.broadcasted_iota(jnp.int32, shape, key_dim)
    query_place = query_block * block_rows + lax.broadcasted_iota(jnp.int32, shape, 1 - key_dim)
    begin = jnp.zeros(shape, jnp.int32)
    for start in starts:
        begin = jnp.where(start <= query_place, start, begin)
    allowed = (key_place <= query_place) & (key_place >= begin)
    return jnp.where(allowed, 0.0, MASKED)


def shared_key_tile(rope_rows, block_rows):
    place = lax.broadcasted_iota(jnp.int32, (ROPE, HEAD), 0)
    lane = lax.broadcasted_iota(jnp.int32, (ROPE, HEAD), 1)
    eye = jnp.where(place == lane, 1.0, 0.0).astype(jnp.bfloat16)
    tile = dot_nn(rope_rows, eye)
    lanes = lax.broadcasted_iota(jnp.int32, (block_rows, HEAD), 1)
    ones = (lanes >= FOLD_AT) & (lanes < FOLD_AT + 3)
    return jnp.where(ones, 1.0, tile).astype(jnp.bfloat16)


def head_window(h):
    at = h * (NOPE + ROPE)
    return at // HEAD * HEAD, at % HEAD


def window_columns(heads):
    return head_window(heads - 1)[0] + WIDE


def head_groups(heads):
    return [(h, min(h + 2, heads)) for h in range(0, heads, 2)]


def forward_kernel(
    blocks, heads, block_map, lengths, qx, lat, wkvb, o_out, ob_out, u_out,
    wkvt, xs, xr, vt, top, acc, bias, s_ref, p_ref,
):
    block_rows = bias.shape[0]
    q_blocks = qx.shape[0]
    starts = starts_of(lengths)
    own = [block_map[j, lax.axis_index("ctx")] for j in range(q_blocks)]
    for first, last in head_groups(heads):
        wkvt[first * HEAD : last * HEAD, :] = (
            wkvb[:, first * HEAD : last * HEAD].astype(jnp.float32).T.astype(jnp.bfloat16)
        )
    top[...] = jnp.full(top.shape, MASKED, jnp.float32)
    vt[:, VDIM:, :] = jnp.ones((heads, SUM_ROWS, block_rows), jnp.bfloat16)
    acc[...] = jnp.zeros(acc.shape, jnp.float32)

    def pair(j, masked):
        def one(h):
            keys = jnp.concatenate([xs[h], xr[...]], axis=1)
            s_ref[h % 3] = dot_nt(keys, qx[j, h])

        def weigh(h):
            old = top[j, h]
            new = old
            for k in range(0, block_rows, 128):
                part = s_ref[h % 3, k : k + 128, :]
                if masked:
                    part = part + bias[k : k + 128, :]
                    s_ref[h % 3, k : k + 128, :] = part
                new = jnp.maximum(new, jnp.max(part, axis=0, keepdims=True))
            fade = jnp.exp2((old - new) * EXP2_SCALE)
            top[j, h] = new
            for k in range(0, block_rows, 128):
                terms = jnp.exp2((s_ref[h % 3, k : k + 128, :] - new) * EXP2_SCALE)
                p_ref[h % 3, k : k + 128, :] = terms.astype(jnp.bfloat16)
            return fade

        def add(h, fade):
            acc[j, h] = fade * acc[j, h] + dot_nn(vt[h], p_ref[h % 3])

        one(0)
        if heads > 1:
            one(1)
        fades = {}
        for h in range(heads):
            if h + 2 < heads:
                one(h + 2)
            fades[h] = weigh(h)
            if h > 1:
                add(h - 2, fades[h - 2])
        for h in range(max(heads - 2, 0), heads):
            add(h, fades[h])

    def step(r, carry):
        key_block = block_map[lax.rem(r, 2), lax.div(r, 2)]
        kinds = [pair_kind(key_block, own[j], starts, block_rows) for j in range(q_blocks)]
        wanted = functools.reduce(jnp.logical_or, [k[0] for k in kinds])

        @pl.when(wanted)
        def _():
            here = pl.ds(pl.multiple_of(r * block_rows, block_rows), block_rows)
            latent = lat[here, :KVR]
            xr[...] = shared_key_tile(lat[here, KVR : KVR + ROPE], block_rows)
            for first, last in head_groups(heads):
                keys = dot_nn(latent, wkvb[:, first * HEAD : last * HEAD]).astype(jnp.bfloat16)
                values = dot_nt(wkvt[first * HEAD : last * HEAD, :], latent).astype(jnp.bfloat16)
                for h in range(first, last):
                    at = (h - first) * HEAD
                    xs[h] = keys[:, at : at + HEAD]
                    vt[h, :VDIM, :] = values[at + NOPE : at + HEAD, :]

        for j in range(q_blocks):
            needed, whole = kinds[j]

            @pl.when(needed & whole)
            def _():
                pair(j, False)

            @pl.when(needed & jnp.logical_not(whole))
            def _():
                bias[...] = mask_bias(key_block, own[j], starts, block_rows, True)
                pair(j, True)

        return carry

    lax.fori_loop(0, blocks, step, 0)
    for j in range(q_blocks):
        here = pl.ds(j * block_rows, block_rows)
        for first, last in head_groups(heads):
            parts = []
            for h in range(first, last):
                total = acc[j, h, VDIM : VDIM + 1, :]
                parts.append(acc[j, h, :VDIM, :] * (1.0 / total))
                u_out[j, h : h + 1, :] = top[j, h] + jnp.log2(total) * (1.0 / EXP2_SCALE)
            if len(parts) == 1:
                parts.append(jnp.zeros_like(parts[0]))
            both = jnp.concatenate(parts, axis=0).T
            width = (last - first) * VDIM
            o_out[here, first * VDIM : first * VDIM + width] = both[:, :width]
            ob_out[here, first * VDIM : first * VDIM + width] = both[:, :width].astype(jnp.bfloat16)


def attention_forward(block_map, lengths, qx, lat, wkvb):
    q_blocks, heads, block_rows, _ = qx.shape
    blocks = lat.shape[0] // block_rows
    rows = q_blocks * block_rows
    vmem = pl.BlockSpec(memory_space=pltpu.VMEM)
    smem = pl.BlockSpec(memory_space=pltpu.SMEM)
    pairs = q_blocks * blocks * heads // 2
    return pl.pallas_call(
        functools.partial(forward_kernel, blocks, heads),
        out_shape=(
            jax.ShapeDtypeStruct((rows, heads * VDIM), jnp.float32),
            jax.ShapeDtypeStruct((rows, heads * VDIM), jnp.bfloat16),
            jax.ShapeDtypeStruct((q_blocks, 16 * -(-heads // 16), block_rows), jnp.float32),
        ),
        in_specs=[smem] * 2 + [vmem] * 3,
        out_specs=(vmem,) * 3,
        scratch_shapes=[
            pltpu.VMEM((heads * HEAD, KVR), jnp.bfloat16),
            pltpu.VMEM((heads, block_rows, HEAD), jnp.bfloat16),
            pltpu.VMEM((block_rows, HEAD), jnp.bfloat16),
            pltpu.VMEM((heads, VDIM + SUM_ROWS, block_rows), jnp.bfloat16),
            pltpu.VMEM((q_blocks, heads, 1, block_rows), jnp.float32),
            pltpu.VMEM((q_blocks, heads, VDIM + SUM_ROWS, block_rows), jnp.float32),
            pltpu.VMEM((block_rows, block_rows), jnp.float32),
            pltpu.VMEM((3, block_rows, block_rows), jnp.float32),
            pltpu.VMEM((3, block_rows, block_rows), jnp.bfloat16),
        ],
        compiler_params=pltpu.CompilerParams(vmem_limit_bytes=VMEM_LIMIT),
        cost_estimate=pl.CostEstimate(
            flops=pairs * 4 * block_rows * block_rows * WIDE,
            bytes_accessed=16 * 1024 * 1024,
            transcendentals=pairs * block_rows * block_rows,
        ),
        name="attention_forward",
    )(block_map, lengths, qx, lat, wkvb)


def three_terms(column):
    first = column.astype(jnp.bfloat16).astype(jnp.float32)
    rest = column - first
    second = rest.astype(jnp.bfloat16).astype(jnp.float32)
    return first, second, rest - second


def fold_in(tile, column, lane):
    for k, term in enumerate(three_terms(column)):
        tile = jnp.where(lane == FOLD_AT + k, term, tile)
    return tile


def backward_kernel(
    blocks, heads, block_map, lengths, qx, qt, u_in, o_in, dob, lat, wkvb, cos, sin,
    dq_out, dlat, gkvb, xs, xr, qo, dt, dq, dkv, dkpe, gsum, bias, flat, s_ref, p_ref, d_ref,
):
    block_rows = bias.shape[0]
    q_blocks = qx.shape[0]
    starts = starts_of(lengths)
    own = [block_map[j, lax.axis_index("ctx")] for j in range(q_blocks)]
    lane = lax.broadcasted_iota(jnp.int32, (block_rows, HEAD), 1)
    for j in range(q_blocks):
        here = pl.ds(j * block_rows, block_rows)
        logs = u_in[j].T
        for first, last in head_groups(heads):
            d_pair = dob[here, first * VDIM : first * VDIM + HEAD].astype(jnp.float32)
            weighted = d_pair * o_in[here, first * VDIM : first * VDIM + HEAD]
            turned = pltpu.roll(d_pair, VDIM, 1)
            for h in range(first, last):
                mine = lane < VDIM if h == first else lane >= VDIM
                delta = jnp.sum(jnp.where(mine, weighted, 0.0), axis=1, keepdims=True)
                d_head = jnp.where(lane >= VDIM, turned if h == first else d_pair, 0.0)
                q_second = qx[j, h, :, HEAD:].astype(jnp.float32)
                qo[j, h, :block_rows, :HEAD] = qx[j, h, :, :HEAD]
                qo[j, h, :block_rows, HEAD:] = fold_in(q_second, -logs[:, h : h + 1], lane).astype(
                    jnp.bfloat16
                )
                qo[j, h, block_rows:, :HEAD] = d_head.astype(jnp.bfloat16)
                qo[j, h, block_rows:, HEAD:] = fold_in(
                    jnp.zeros((block_rows, HEAD), jnp.float32), -delta, lane
                ).astype(jnp.bfloat16)
                dt[j, h] = d_head.T[VDIM:, :].astype(jnp.bfloat16)
    dq[...] = jnp.zeros(dq.shape, jnp.float32)
    gsum[...] = jnp.zeros(gsum.shape, jnp.float32)

    def pair(j, masked):
        def raw(h):
            keys = jnp.concatenate([xs[h], xr[...]], axis=1)
            s_ref[h % 2] = dot_nt(qo[j, h], keys)

        def weigh(h):
            for k in range(0, block_rows, 128):
                scores = s_ref[h % 2, k : k + 128, :] * EXP2_SCALE
                if masked:
                    scores = scores + bias[k : k + 128, :]
                probs = jnp.exp2(scores)
                p_ref[h % 2, k : k + 128, :] = probs.astype(jnp.bfloat16)
                d_ref[h % 2, k : k + 128, :] = (
                    probs * s_ref[h % 2, block_rows + k : block_rows + k + 128, :]
                ).astype(jnp.bfloat16)

        def add(h):
            keys = jnp.concatenate([xs[h], xr[...]], axis=1)
            d_scores = d_ref[h % 2]
            dq[j, h] += dot_nn(d_scores, keys)
            d_keys = dot_nn(qt[j, h], d_scores)
            dkv[h, :NOPE, :] += d_keys[:NOPE]
            dkpe[...] += d_keys[NOPE:]
            dkv[h, NOPE:, :] += dot_nn(dt[j, h], p_ref[h % 2])

        raw(0)
        for h in range(heads):
            if h + 1 < heads:
                raw(h + 1)
            weigh(h)
            if h:
                add(h - 1)
        add(heads - 1)

    def step(r, carry):
        key_block = block_map[lax.rem(r, 2), lax.div(r, 2)]
        kinds = [pair_kind(key_block, own[j], starts, block_rows) for j in range(q_blocks)]
        wanted = functools.reduce(jnp.logical_or, [k[0] for k in kinds])
        here = pl.ds(pl.multiple_of(r * block_rows, block_rows), block_rows)

        @pl.when(wanted)
        def _():
            latent = lat[here, :KVR]
            xr[...] = shared_key_tile(lat[here, KVR : KVR + ROPE], block_rows)
            for first, last in head_groups(heads):
                keys = dot_nn(latent, wkvb[:, first * HEAD : last * HEAD]).astype(jnp.bfloat16)
                for h in range(first, last):
                    xs[h] = keys[:, (h - first) * HEAD : (h - first + 1) * HEAD]
            dkv[...] = jnp.zeros(dkv.shape, jnp.float32)
            dkpe[...] = jnp.zeros(dkpe.shape, jnp.float32)

        for j in range(q_blocks):
            needed, whole = kinds[j]

            @pl.when(needed & whole)
            def _():
                pair(j, False)

            @pl.when(needed & jnp.logical_not(whole))
            def _():
                bias[...] = mask_bias(key_block, own[j], starts, block_rows, False)
                pair(j, True)

        @pl.when(wanted)
        def _():
            latent = lat[here, :KVR]
            d_latent = jnp.zeros((KVR, block_rows), jnp.float32)
            for h in range(heads):
                d_head = jnp.concatenate(
                    [dkv[h, :NOPE, :] * SCORE_SCALE, dkv[h, NOPE:, :]], axis=0
                ).astype(jnp.bfloat16)
                d_latent += dot_nn(wkvb[:, h * HEAD : (h + 1) * HEAD], d_head)
                gsum[h * HEAD : (h + 1) * HEAD, :] += dot_nn(d_head, latent)
            dlat[here, :KVR] = d_latent.T.astype(jnp.bfloat16)
            rope = jnp.concatenate(
                [dkpe[...] * SCORE_SCALE, jnp.zeros((HEAD - ROPE, block_rows), jnp.float32)], axis=0
            )
            dlat[here, KVR:] = rope.T[:, :ROPE].astype(jnp.bfloat16)

        @pl.when(jnp.logical_not(wanted))
        def _():
            dlat[here, :] = jnp.zeros((block_rows, KVR + ROPE), jnp.bfloat16)

        return carry

    lax.fori_loop(0, blocks, step, 0)
    for h in range(heads):
        gkvb[:, h * HEAD : (h + 1) * HEAD] = gsum[h * HEAD : (h + 1) * HEAD, :].T.astype(
            jnp.bfloat16
        )
    for j in range(q_blocks):
        here = pl.ds(j * block_rows, block_rows)
        cos_j, sin_j = cos[here, :], sin[here, :]
        flat[...] = jnp.zeros(flat.shape, jnp.float32)
        for h in range(heads):
            nope = jnp.where(lane < NOPE, dq[j, h, :, :HEAD], 0.0)
            rope = dq[j, h, :, HEAD:]
            shifted = rope * sin_j
            left = pltpu.roll(shifted, HEAD - ROPE // 2, 1)
            right = pltpu.roll(shifted, ROPE // 2, 1)
            swapped = jnp.where(lane < ROPE // 2, left, jnp.where(lane < ROPE, -right, 0.0))
            back = pltpu.roll(jnp.where(lane < ROPE, rope * cos_j + swapped, 0.0), NOPE, 1)
            whole = jnp.concatenate([(nope + back) * SCORE_SCALE, jnp.zeros_like(nope)], axis=1)
            at, shift = head_window(h)
            flat[:, at : at + WIDE] += pltpu.roll(whole, shift, 1)
        dq_out[here, :] = flat[:, : heads * (NOPE + ROPE)].astype(jnp.bfloat16)


def attention_backward(block_map, lengths, qx, qt, u_in, o_in, dob, lat, wkvb, cos, sin):
    q_blocks, heads, block_rows, _ = qx.shape
    blocks = lat.shape[0] // block_rows
    rows = q_blocks * block_rows
    odd = -(heads * VDIM) % HEAD
    if odd:
        o_in = jnp.pad(o_in, ((0, 0), (0, odd)))
        dob = jnp.pad(dob, ((0, 0), (0, odd)))
    vmem = pl.BlockSpec(memory_space=pltpu.VMEM)
    smem = pl.BlockSpec(memory_space=pltpu.SMEM)
    pairs = q_blocks * blocks * heads // 2
    return pl.pallas_call(
        functools.partial(backward_kernel, blocks, heads),
        out_shape=(
            jax.ShapeDtypeStruct((rows, heads * (NOPE + ROPE)), jnp.bfloat16),
            jax.ShapeDtypeStruct((lat.shape[0], KVR + ROPE), jnp.bfloat16),
            jax.ShapeDtypeStruct((KVR, heads * HEAD), jnp.bfloat16),
        ),
        in_specs=[smem] * 2 + [vmem] * 9,
        out_specs=(vmem,) * 3,
        scratch_shapes=[
            pltpu.VMEM((heads, block_rows, HEAD), jnp.bfloat16),
            pltpu.VMEM((block_rows, HEAD), jnp.bfloat16),
            pltpu.VMEM((q_blocks, heads, 2 * block_rows, WIDE), jnp.bfloat16),
            pltpu.VMEM((q_blocks, heads, VDIM, block_rows), jnp.bfloat16),
            pltpu.VMEM((q_blocks, heads, block_rows, WIDE), jnp.float32),
            pltpu.VMEM((heads, HEAD, block_rows), jnp.float32),
            pltpu.VMEM((ROPE, block_rows), jnp.float32),
            pltpu.VMEM((heads * HEAD, KVR), jnp.float32),
            pltpu.VMEM((block_rows, block_rows), jnp.float32),
            pltpu.VMEM((block_rows, window_columns(heads)), jnp.float32),
            pltpu.VMEM((2, 2 * block_rows, block_rows), jnp.float32),
            pltpu.VMEM((2, block_rows, block_rows), jnp.bfloat16),
            pltpu.VMEM((2, block_rows, block_rows), jnp.bfloat16),
        ],
        compiler_params=pltpu.CompilerParams(vmem_limit_bytes=VMEM_LIMIT),
        cost_estimate=pl.CostEstimate(
            flops=pairs * 8 * block_rows * block_rows * WIDE,
            bytes_accessed=24 * 1024 * 1024,
            transcendentals=pairs * block_rows * block_rows,
        ),
        name="attention_backward",
    )(block_map, lengths, qx, qt, u_in, o_in, dob, lat, wkvb, cos, sin)


MESH = pl.DeviceIdType.MESH


class LineSum:
    def __init__(self, n, own, landing, total, sems, lag):
        self.n, self.own, self.landing, self.total, self.lag = n, own, landing, total, lag
        self.up_send, self.up_land, self.down_send, self.back_send, self.down_land = sems
        self.me = lax.axis_index("tp")
        self.root = (n - 1) // 2
        self.chunks = own.shape[0]
        self.has_left, self.has_right = self.me > 0, self.me < n - 1
        self.root_lag = (n - 1 - self.root) * lag
        self.land_lag = 2 * self.root_lag
        self.ticks = self.chunks + self.land_lag

    def greet(self, barrier):
        me = self.me
        for there, other in ((self.has_left, me - 1), (self.has_right, me + 1)):

            @pl.when(there)
            def _(other=other):
                pl.semaphore_signal(barrier, inc=1, device_id={"tp": other}, device_id_type=MESH)

    def wait_greetings(self, barrier, others):
        both = self.has_left & self.has_right

        @pl.when(both)
        def _():
            pl.semaphore_wait(barrier, 2 + others)

        @pl.when(jnp.logical_not(both))
        def _():
            pl.semaphore_wait(barrier, 1 + others)

    def copy_to(self, source, target, send, land, c, other):
        return pltpu.make_async_remote_copy(
            src_ref=source.at[c],
            dst_ref=target.at[c],
            send_sem=send.at[c],
            recv_sem=land.at[c],
            device_id={"tp": other},
            device_id_type=MESH,
        )

    def rise_left(self, c):
        return self.copy_to(self.own, self.landing, self.up_send, self.up_land, c, self.me + 1)

    def rise_right(self, c):
        return self.copy_to(self.own, self.landing, self.up_send, self.up_land, c, self.me - 1)

    def rise_last(self, c):
        return self.copy_to(self.own, self.total, self.up_send, self.down_land, c, self.me - 1)

    def fall_right(self, c):
        return self.copy_to(self.total, self.total, self.down_send, self.down_land, c, self.me + 1)

    def fall_left(self, c):
        return self.copy_to(self.total, self.total, self.back_send, self.down_land, c, self.me - 1)

    def rise(self, c):
        me, root = self.me, self.root
        rises = [(me == root + 1, self.rise_last)]
        if root:
            rises.append((me < root, self.rise_left))
        if self.n - 1 > root + 1:
            rises.append((me > root + 1, self.rise_right))
        for who, copy in rises:

            @pl.when(who)
            def _(copy=copy):
                copy(c).start()

    def inside(self, c):
        return (c >= 0) & (c < self.chunks)

    def added(self, refs, c):
        sums = refs[0][c].astype(jnp.float32)
        for ref in refs[1:]:
            sums = sums + ref[c].astype(jnp.float32)
        return sums.astype(self.total.dtype)

    def leaf(self, c):
        is_leaf = self.me == self.n - 1
        if self.root:
            is_leaf = is_leaf | (self.me == 0)

        @pl.when(is_leaf & self.inside(c))
        def _():
            self.rise(c)

    def leaves(self):
        def body(c, carry):
            self.leaf(c)
            return carry

        lax.fori_loop(0, self.chunks, body, 0)

    def pump(self, first, last):
        def body(t, carry):
            self.duty(t)
            return carry

        lax.fori_loop(first, last, body, 0)

    def duty(self, t):
        me, root = self.me, self.root
        if self.n > 3:
            c = t - self.lag * jnp.where(me < root, me, self.n - 1 - me)

            @pl.when((me != root) & self.has_left & self.has_right & self.inside(c))
            def _():
                self.rise_right(c).wait_recv()
                self.own[c] = self.added([self.own, self.landing], c)
                self.rise(c)

        c_root = t - self.root_lag

        @pl.when((me == root) & self.inside(c_root))
        def _():
            if root:
                self.rise_left(c_root).wait_recv()
            self.fall_right(c_root).wait_recv()
            terms = [self.own, self.landing, self.total] if root else [self.own, self.total]
            self.total[c_root] = self.added(terms, c_root)
            self.fall_right(c_root).start()
            if root:
                self.fall_left(c_root).start()

        c_fall = t - self.root_lag - self.lag * jnp.where(me < root, root - me, me - root)

        @pl.when((me != root) & self.inside(c_fall))
        def _():
            self.fall_right(c_fall).wait_recv()

            @pl.when((me > root) & self.has_right)
            def _():
                self.fall_right(c_fall).start()

            @pl.when((me < root) & self.has_left)
            def _():
                self.fall_left(c_fall).start()

    def landed(self, t):
        return t - self.land_lag

    def drain(self):
        me = self.me

        def body(c, carry):
            @pl.when(me != self.root)
            def _():
                self.rise_right(c).wait_send()

            @pl.when((me >= self.root) & self.has_right)
            def _():
                self.fall_right(c).wait_send()

            @pl.when((me <= self.root) & self.has_left)
            def _():
                self.fall_left(c).wait_send()

            return carry

        lax.fori_loop(0, self.chunks, body, 0)


def line_sems(chunks):
    return [pltpu.SemaphoreType.DMA((chunks,))] * 5


def scatter_blocks(bits_left):
    chips = []
    for value in range(1 << len(bits_left)):
        chip = 0
        for at, bit in enumerate(bits_left):
            chip = chip + (((value >> at) & 1) << (bit - 1))
        chips.append(chip)
    return chips


class Scatter:
    def __init__(self, n, rows, columns, is_given):
        self.n, self.rows, self.columns, self.is_given = n, rows, columns, is_given
        self.count = n.bit_length() - 1
        self.parts = 2 if rows % 32 == 0 else 1

    def scratch(self):
        n, count = self.n, self.count
        half = jnp.bfloat16
        dma = pltpu.SemaphoreType.DMA
        shapes = [pltpu.VMEM((n // 2, self.rows, self.columns), half)]
        if not self.is_given:
            shapes.append(pltpu.VMEM((n // 2, self.rows, self.columns), half))
        for step in range(count - 1):
            shapes.append(pltpu.VMEM((n >> (step + 2), self.rows, self.columns), half))
        shapes += [dma((n // 2,))] * 2
        for step in range(count - 1):
            shapes += [dma((2, n >> (step + 2)))] * 2
        return shapes

    def bind(self, take, source, emit):
        self.held = take(1)[0]
        self.sent = None if self.is_given else take(1)[0]
        self.landed = take(self.count - 1)
        self.core_sems = take(2)
        self.step_sems = [take(2) for _ in range(self.count - 1)]
        self.source, self.emit = source, emit
        self.me = lax.axis_index("ctx")
        self.core = self.me & 1
        self.chips = self.n // 2
        self.orders = (tuple(range(1, self.count)), tuple(range(self.count - 1, 0, -1)))
        self.tiles = [(c, min(c + 512, self.columns)) for c in range(0, self.columns, 512)]
        return self

    def own(self, dest, first, last):
        at = pl.ds(pl.multiple_of(dest * self.rows, 16), self.rows)
        if self.is_given:
            return self.source[at, first:last].astype(jnp.float32)
        return dot_nn(self.source[0][at, :], self.source[1][:, first:last])

    def core_copy(self, chip):
        if self.is_given:
            at = pl.ds(pl.multiple_of((2 * chip + 1 - self.core) * self.rows, 16), self.rows)
            source = self.source.at[at, :]
        else:
            source = self.sent.at[chip]
        return pltpu.make_async_remote_copy(
            src_ref=source,
            dst_ref=self.held.at[chip],
            send_sem=self.core_sems[0].at[chip],
            recv_sem=self.core_sems[1].at[chip],
            device_id={"ctx": self.me ^ 1},
            device_id_type=MESH,
        )

    def step_copies(self, step):
        half = self.rows // self.parts
        me = self.me
        copies = []
        for part, order in enumerate(self.orders[: self.parts]):
            bit = order[step]
            at = pl.ds(part * half, half)
            for slot, free in enumerate(scatter_blocks(sorted(order[step + 1 :]))):
                keep = free + ((me >> bit) & 1) * (1 << (bit - 1))
                send = free + (1 - ((me >> bit) & 1)) * (1 << (bit - 1))
                for b in order[:step]:
                    own = ((me >> b) & 1) * (1 << (b - 1))
                    keep, send = keep + own, send + own
                copy = pltpu.make_async_remote_copy(
                    src_ref=self.held.at[send, at, :],
                    dst_ref=self.landed[step].at[slot, at, :],
                    send_sem=self.step_sems[step][0].at[part, slot],
                    recv_sem=self.step_sems[step][1].at[part, slot],
                    device_id={"ctx": me ^ (1 << bit)},
                    device_id_type=MESH,
                )
                copies.append((copy, keep, slot, at))
        return copies

    def start_core(self, also=None):
        def body(chip, carry):
            if also is not None:
                also(chip)
            if not self.is_given:
                for first, last in self.tiles:
                    self.sent[chip, :, first:last] = self.own(
                        2 * chip + 1 - self.core, first, last
                    ).astype(jnp.bfloat16)
            self.core_copy(chip).start()
            return carry

        lax.fori_loop(0, self.chips, body, 0)

    def finish_core(self, also=None):
        def body(chip, carry):
            if also is not None:
                also(chip)
            self.core_copy(chip).wait_recv()
            for first, last in self.tiles:
                total = self.own(2 * chip + self.core, first, last)
                total = total + self.held[chip, :, first:last].astype(jnp.float32)
                self.held[chip, :, first:last] = total.astype(jnp.bfloat16)
            return carry

        lax.fori_loop(0, self.chips, body, 0)

    def start_step(self, step):
        for copy, _, _, _ in self.step_copies(step):
            copy.start()

    def finish_step(self, step):
        for copy, keep, slot, at in self.step_copies(step):
            copy.wait_recv()
            for first, last in self.tiles:
                total = self.held[keep, at, first:last].astype(jnp.float32)
                total = total + self.landed[step][slot, at, first:last].astype(jnp.float32)
                if step == self.count - 2:
                    self.emit(at, first, last, total)
                else:
                    self.held[keep, at, first:last] = total.astype(jnp.bfloat16)
        if step + 1 < self.count - 1:
            self.start_step(step + 1)

    def drain(self):
        def body(chip, carry):
            self.core_copy(chip).wait_send()
            return carry

        lax.fori_loop(0, self.chips, body, 0)
        for step in range(self.count - 1):
            for copy, _, _, _ in self.step_copies(step):
                copy.wait_send()


def taker(refs):
    refs = list(refs)

    def take(k):
        taken = refs[:k]
        del refs[:k]
        return taken

    return take


def store_in(ref):
    def emit(at, first, last, total):
        ref[at, first:last] = total.astype(ref.dtype)

    return emit


def turn(source, target):
    def body(c, carry):
        at = pl.ds(pl.multiple_of(c * 128, 128), 128)
        target[at, :] = source[:, at].astype(jnp.float32).T.astype(jnp.bfloat16)
        return carry

    lax.fori_loop(0, source.shape[1] // 128, body, 0)


def greet_ctx(n, barrier):
    me = lax.axis_index("ctx")
    count = n.bit_length() - 1
    for bit in range(count):
        pl.semaphore_signal(barrier, inc=1, device_id={"ctx": me ^ (1 << bit)}, device_id_type=MESH)
    return count


def spread(waits, ticks):
    portion = -(-ticks // waits)
    return [(min(k * portion, ticks), min((k + 1) * portion, ticks)) for k in range(waits)]


def gate_up_kernel(
    n, tp, plans, normed, d_gate, d_up, terms, tokens, attn, cot, gain_row, w_out,
    gate_out, up_out, d_attn, d_heads, g_mid, *refs,
):
    take = taker(refs)
    own, landing, sums, normed_t, slots, in_sems, own_sem = take(7)
    line = LineSum(tp, own, landing, sums, take(5), LAG)
    gate = plans[0].bind(take, (normed_t, d_gate), store_in(gate_out))
    up = plans[1].bind(take, (normed_t, d_up), store_in(up_out))
    width = normed.shape[1]
    blocks = normed.shape[0] // BLOCK
    per_block = BLOCK // CHUNK
    load = pltpu.make_async_copy(terms, own, own_sem)
    load.start()
    barrier = pltpu.get_barrier_semaphore()
    others = greet_ctx(n, barrier)
    line.greet(barrier)

    def fetch(b):
        rows = pl.ds(b * BLOCK, BLOCK)
        return [
            pltpu.make_async_copy(
                source.at[rows, :], slots.at[b % 2, k], in_sems.at[b % 2, k]
            )
            for k, source in enumerate((tokens, attn, cot))
        ]

    for b in range(min(2, blocks)):
        for copy in fetch(b):
            copy.start()
    g_mid[...] = jnp.zeros(g_mid.shape, jnp.float32)

    def norm(b):
        for copy in fetch(b):
            copy.wait()
        for part in range(0, BLOCK, 2 * CHUNK):
            rows = pl.ds(b * BLOCK + part, 2 * CHUNK)
            here = pl.ds(part, 2 * CHUNK)
            c = b * per_block + part // CHUNK
            incoming = jnp.concatenate([sums[c], sums[c + 1]], axis=0).astype(jnp.float32)
            middle = slots[b % 2, 0, here, :].astype(jnp.float32)
            middle = middle + RESIDUAL_SCALE * slots[b % 2, 1, here, :].astype(jnp.float32)
            d_norm, gain_terms = norm_back(
                incoming, middle, norm_scale(middle), gain_row[:, width : 2 * width]
            )
            g_mid[...] += gain_terms
            total = slots[b % 2, 2, here, :].astype(jnp.float32) + d_norm
            d_attn[rows, :] = (RESIDUAL_SCALE * total).astype(jnp.bfloat16)
        rows = pl.ds(b * BLOCK, BLOCK)
        d_heads[rows, :] = dot_nn(d_attn[rows, :], w_out[...]).astype(jnp.bfloat16)
        if b + 2 < blocks:
            for copy in fetch(b + 2):
                copy.start()

    load.wait()
    line.wait_greetings(barrier, others)
    line.leaves()
    turn(normed, normed_t)
    chips = n // 2
    gate.start_core()
    gate.finish_core(line.duty)
    gate.start_step(0)
    up.start_core(lambda chip: line.duty(chips + chip))
    up.finish_core(lambda chip: line.duty(2 * chips + chip))
    up.start_step(0)
    steps = [(item, step) for step in range(gate.count - 1) for item in (gate, up)]
    done = 3 * chips
    next_block = 0
    for (item, step), (first, last) in zip(steps, spread(len(steps), line.ticks - done)):
        line.pump(done + first, done + last)
        while next_block < blocks and line.landed(done + last - 1) >= (next_block + 1) * per_block - 1:
            norm(next_block)
            next_block += 1
        item.finish_step(step)
    for item in (gate, up, line):
        item.drain()


def gate_up_grads(
    n, tp, normed, d_gate, d_up, terms, tokens, attn, cot, gain_row, w_out, collective_id
):
    rows, width = normed.shape
    hidden = d_gate.shape[1]
    head_width = w_out.shape[1]
    vmem = pl.BlockSpec(memory_space=pltpu.VMEM)
    anywhere = pl.BlockSpec(memory_space=pl.ANY)
    half = jnp.bfloat16
    plans = [Scatter(n, width // n, hidden, False) for _ in range(2)]
    chunked = (rows // CHUNK, CHUNK, width)
    return pl.pallas_call(
        functools.partial(gate_up_kernel, n, tp, plans),
        out_shape=(
            jax.ShapeDtypeStruct((width // n, hidden), half),
            jax.ShapeDtypeStruct((width // n, hidden), half),
            jax.ShapeDtypeStruct((rows, width), half),
            jax.ShapeDtypeStruct((rows, head_width), half),
            jax.ShapeDtypeStruct((1, width), jnp.float32),
        ),
        in_specs=[vmem] * 3 + [anywhere] * 4 + [vmem] * 2,
        out_specs=(vmem,) * 5,
        scratch_shapes=[
            pltpu.VMEM(chunked, half),
            pltpu.VMEM(chunked, half),
            pltpu.VMEM(chunked, half),
            pltpu.VMEM((width, rows), half),
            pltpu.VMEM((2, 3, BLOCK, width), half),
            pltpu.SemaphoreType.DMA((2, 3)),
            pltpu.SemaphoreType.DMA,
            *line_sems(rows // CHUNK),
            *plans[0].scratch(),
            *plans[1].scratch(),
        ],
        compiler_params=pltpu.CompilerParams(
            vmem_limit_bytes=MIDDLE_VMEM, collective_id=collective_id, has_side_effects=True
        ),
        cost_estimate=pl.CostEstimate(
            flops=2 * rows * width * (2 * hidden + head_width),
            bytes_accessed=28 * 1024 * 1024,
            transcendentals=0,
        ),
        name=f"gate_up_grads_{collective_id}",
    )(normed, d_gate, d_up, terms.reshape(chunked), tokens, attn, cot, gain_row, w_out)


class FeedSum:
    def __init__(self, tp, take, at, chunks, terms, tokens, attn, out):
        own, landing, sums, self.tokens, self.attn, sems = take(6)
        self.out = out
        some = pl.ds(at, chunks)
        pairs = ((terms, own), (tokens, self.tokens), (attn, self.attn))
        self.loads = [
            pltpu.make_async_copy(source.at[some], target, sems.at[k])
            for k, (source, target) in enumerate(pairs)
        ]
        self.line = LineSum(tp, own, landing, sums, take(5), LAG)
        self.ticks = self.line.ticks

    def load(self):
        for load in self.loads:
            load.start()

    def begin(self):
        for load in self.loads:
            load.wait()
        self.line.leaves()

    def duty(self, t):
        self.line.duty(t)
        c = self.line.landed(t)

        @pl.when(self.line.inside(c))
        def _():
            both = self.attn[c].astype(jnp.float32) + self.line.total[c].astype(jnp.float32)
            total = self.tokens[c].astype(jnp.float32) + RESIDUAL_SCALE * both
            self.out[c] = total.astype(jnp.bfloat16)

    def pump(self, first, last):
        def body(t, carry):
            self.duty(t)
            return carry

        lax.fori_loop(first, last, body, 0)


def feed_scratch(chunks, width):
    return [pltpu.VMEM((chunks, CHUNK, width), jnp.bfloat16)] * 5 + [
        pltpu.SemaphoreType.DMA((3,)),
        *line_sems(chunks),
    ]


TAIL_CHUNK = 64


def up_tail_kernel(
    n, tp, plans, feed_chunks, d_lat, d_query, w_qb, g_kvb, d_attn, ob, q_latent, d_feed, act,
    f_part, tokens, attn, sum_q, sum_lat, down_out, out_out, qb_out, kvb_out, layer_out, *refs,
):
    take = taker(refs)
    own_q, land_q, own_lat, land_lat, d_attn_t, q_latent_t, d_feed_t = take(7)
    line_q = LineSum(tp, own_q, land_q, sum_q, take(5), LAG)
    line_lat = LineSum(tp, own_lat, land_lat, sum_lat, take(5), LAG)
    feed = FeedSum(tp, take, 0, feed_chunks, f_part, tokens, attn, layer_out)
    feed.load()
    chunk = own_q.shape[1]

    def store_lat(at, first, last, total):
        for k in range(at.size // chunk):
            own_lat[at.start // chunk + k, :, first:last] = total[
                k * chunk : (k + 1) * chunk
            ].astype(jnp.bfloat16)

    lat, down, out, qb, kvb = plans
    lat.bind(take, d_lat, store_lat)
    down.bind(take, (d_feed_t, act), store_in(down_out))
    out.bind(take, (d_attn_t, ob), store_in(out_out))
    qb.bind(take, (q_latent_t, d_query), store_in(qb_out))
    kvb.bind(take, g_kvb, store_in(kvb_out))
    barrier = pltpu.get_barrier_semaphore()
    others = greet_ctx(n, barrier)
    line_q.greet(barrier)
    line_q.wait_greetings(barrier, others)
    lat.start_core()

    def query(c, carry):
        rows = pl.ds(pl.multiple_of(c * 2 * chunk, 2 * chunk), 2 * chunk)
        part = dot_nn(d_query[rows, :], w_qb[...]).astype(jnp.bfloat16)
        for k in range(2):
            own_q[2 * c + k] = part[k * chunk : (k + 1) * chunk]
            line_q.leaf(2 * c + k)
        return carry

    lax.fori_loop(0, own_q.shape[0] // 2, query, 0)
    lat.finish_core()
    lat.start_step(0)
    turn(d_feed, d_feed_t)
    down.start_core()
    lat.finish_step(0)
    down.finish_core()
    for step in range(1, lat.count - 1):
        lat.finish_step(step)
    line_lat.leaves()
    down.start_step(0)
    feed.begin()
    chips = n // 2
    turn(d_attn, d_attn_t)
    out.start_core(line_q.duty)
    out.finish_core(lambda chip: line_q.duty(chips + chip))
    out.start_step(0)
    kvb.start_core()
    turn(q_latent, q_latent_t)
    qb.start_core(lambda chip: line_q.duty(2 * chips + chip))
    kvb.finish_core()
    kvb.start_step(0)
    qb.finish_core(line_lat.duty)
    qb.start_step(0)
    steps = [(item, step) for step in range(lat.count - 1) for item in (down, out, kvb, qb)]
    q_share = spread(len(steps), line_q.ticks - 3 * chips)
    lat_share = spread(len(steps), line_lat.ticks - chips)
    feed_share = spread(len(steps), feed.ticks)
    for (item, step), (a, b), (c, d), (e, f) in zip(steps, q_share, lat_share, feed_share):
        line_q.pump(3 * chips + a, 3 * chips + b)
        line_lat.pump(chips + c, chips + d)
        feed.pump(e, f)
        item.finish_step(step)
    for item in (*plans, line_q, line_lat, feed.line):
        item.drain()


def up_tail(
    n, tp, d_lat, d_query, w_qb, g_kvb, d_attn, ob, q_latent, d_feed, act, f_part, tokens, attn,
    feed_chunks, collective_id,
):
    rows, width = d_attn.shape
    rank = q_latent.shape[1]
    hidden = act.shape[1]
    lat_width = d_lat.shape[1]
    vmem = pl.BlockSpec(memory_space=pltpu.VMEM)
    half = jnp.bfloat16
    plans = [
        Scatter(n, rows, lat_width, True),
        Scatter(n, width // n, hidden, False),
        Scatter(n, width // n, ob.shape[1], False),
        Scatter(n, rank // n, d_query.shape[1], False),
        Scatter(n, KVR // n, g_kvb.shape[1], True),
    ]
    q_shape = (rows // TAIL_CHUNK, TAIL_CHUNK, rank)
    lat_shape = (rows // TAIL_CHUNK, TAIL_CHUNK, lat_width)
    anywhere = pl.BlockSpec(memory_space=pl.ANY)
    chunked = (-1, CHUNK, width)
    sum_q, sum_lat, *grads, layer_out = pl.pallas_call(
        functools.partial(up_tail_kernel, n, tp, plans, feed_chunks),
        out_shape=(
            jax.ShapeDtypeStruct(q_shape, half),
            jax.ShapeDtypeStruct(lat_shape, half),
            *[jax.ShapeDtypeStruct((plan.rows, plan.columns), half) for plan in plans[1:]],
            jax.ShapeDtypeStruct((feed_chunks, CHUNK, width), half),
        ),
        in_specs=[vmem] * 9 + [anywhere] * 3,
        out_specs=(vmem,) * 7,
        scratch_shapes=[
            pltpu.VMEM(q_shape, half),
            pltpu.VMEM(q_shape, half),
            pltpu.VMEM(lat_shape, half),
            pltpu.VMEM(lat_shape, half),
            pltpu.VMEM((width, rows), half),
            pltpu.VMEM((rank, rows), half),
            pltpu.VMEM((width, rows), half),
            *line_sems(rows // TAIL_CHUNK),
            *line_sems(rows // TAIL_CHUNK),
            *feed_scratch(feed_chunks, width),
            *[shape for plan in plans for shape in plan.scratch()],
        ],
        compiler_params=pltpu.CompilerParams(
            vmem_limit_bytes=MIDDLE_VMEM, collective_id=collective_id, has_side_effects=True
        ),
        cost_estimate=pl.CostEstimate(
            flops=2 * rows * width * (hidden + ob.shape[1]) + 4 * rows * rank * d_query.shape[1],
            bytes_accessed=32 * 1024 * 1024,
            transcendentals=0,
        ),
        name=f"up_tail_{collective_id}",
    )(
        d_lat,
        d_query,
        w_qb,
        g_kvb,
        d_attn,
        ob,
        q_latent,
        d_feed,
        act,
        *[array.reshape(chunked) for array in (f_part, tokens, attn)],
    )
    return (
        sum_q.reshape(rows, rank),
        sum_lat.reshape(rows, lat_width),
        *grads,
        layer_out.reshape(-1, width),
    )


def down_tail_kernel(
    n, tp, plans, feed_chunks, sum_q, sum_lat, q_pre, lat_raw, tokens, d_attn, gain_row, g_mid, w_qa,
    w_kva, cos, sin, f_part, tokens_chunked, attn, grad_in, qa_out, kva_out, gains_out, layer_out,
    d_q, d_kv, normed_t, scales, g_in, g_q, g_kv, packed, packing, grad_slots, out_sems, *refs,
):
    take = taker(refs)
    qa, kva, gains = plans
    qa.bind(take, (normed_t, d_q), store_in(qa_out))
    kva.bind(take, (normed_t, d_kv), store_in(kva_out))
    gains.bind(take, packed, store_in(gains_out))
    at = f_part.shape[0] - feed_chunks
    feed = FeedSum(tp, take, at, feed_chunks, f_part, tokens_chunked, attn, layer_out)
    feed.load()
    rows = tokens.shape[0]
    block = rows // 4
    gain_in, _, gain_q, gain_kv = split_gains(gain_row, tokens.shape[1], q_pre.shape[1])
    lane = lax.broadcasted_iota(jnp.int32, (block, HEAD), 1)
    barrier = pltpu.get_barrier_semaphore()
    others = greet_ctx(n, barrier)
    feed.line.greet(barrier)

    def rows_of(k):
        return pl.ds(pl.multiple_of(k * block, block), block)

    def deliver(k, slot):
        return pltpu.make_async_copy(
            grad_slots.at[slot], grad_in.at[rows_of(k), :], out_sems.at[slot]
        )

    feed.line.wait_greetings(barrier, others)
    feed.begin()
    for ref in (g_in, g_q, g_kv):
        ref[...] = jnp.zeros(ref.shape, jnp.float32)

    def norms(k, carry):
        at = rows_of(k)
        pre = q_pre[at, :]
        d_pre, terms = norm_back(
            sum_q[at, :].astype(jnp.float32), pre, norm_scale(pre), gain_q
        )
        g_q[...] += terms
        d_q[at, :] = d_pre.astype(jnp.bfloat16)
        raw = lat_raw[at, :]
        d_raw, terms = norm_back(
            sum_lat[at, :KVR].astype(jnp.float32), raw, norm_scale(raw), gain_kv
        )
        g_kv[...] += terms
        d_kv[at, :KVR] = d_raw.astype(jnp.bfloat16)
        rope = sum_lat[at, KVR:].astype(jnp.float32)
        rope = jnp.concatenate([rope, jnp.zeros((block, HEAD - ROPE), jnp.float32)], axis=1)
        rope = rope_tile_back(rope, cos[at, :], sin[at, :], lane)
        d_kv[at, KVR:] = rope[:, :ROPE].astype(jnp.bfloat16)
        values = tokens[at, :].astype(jnp.float32)
        scale = norm_scale(values)
        scales[at, :] = jnp.broadcast_to(scale, (block, HEAD))
        normed = values * scale * gain_in
        for c in range(0, normed.shape[1], 128):
            normed_t[c : c + 128, at] = normed[:, c : c + 128].T.astype(jnp.bfloat16)
        return carry

    lax.fori_loop(0, 4, norms, 0)
    chips = n // 2
    qa.start_core()
    kva.start_core()
    qa.finish_core()
    qa.start_step(0)
    kva.finish_core(feed.duty)
    kva.start_step(0)
    shares = [(chips + a, chips + b) for a, b in spread(4 + 3, feed.ticks - chips)]
    for k in range(4):
        at = pl.ds(k * block, block)
        feed.pump(*shares[k])
        if k >= 2:
            deliver(k - 2, k % 2).wait()
        d_normed = dot_nt(d_q[at, :], w_qa[...]) + dot_nn(d_kv[at, :], w_kva[...])
        d_values, terms = norm_back(
            d_normed, tokens[at, :].astype(jnp.float32), scales[at, :1], gain_in
        )
        g_in[...] += terms
        d_middle = d_attn[at, :].astype(jnp.float32) * (1.0 / RESIDUAL_SCALE)
        grad_slots[k % 2] = d_middle + d_values
        deliver(k, k % 2).start()
    packing[...] = jnp.zeros(packing.shape, jnp.float32)
    lines = gains.rows
    at = 0
    for whole in (g_in, g_mid, g_q, g_kv):
        share = whole.shape[1] // n
        piece = 32 if share % 32 == 0 else 16
        for dest in range(n):
            for place in range(0, share, piece):
                row, column = divmod(at + place, HEAD)
                row += dest * lines
                first = dest * share + place
                packing[row : row + 1, column : column + piece] = whole[:, first : first + piece]
        at += share
    packed[...] = packing[...].astype(jnp.bfloat16)
    gains.start_core()
    feed.pump(*shares[4])
    gains.finish_core()
    gains.start_step(0)
    feed.pump(*shares[5])
    feed.pump(*shares[6])
    for step in range(qa.count - 1):
        for item in (qa, kva, gains):
            item.finish_step(step)
    deliver(2, 0).wait()
    deliver(3, 1).wait()
    for item in (*plans, feed.line):
        item.drain()


def down_tail(
    n, tp, sum_q, sum_lat, q_pre, lat_raw, tokens, d_attn, gain_row, g_mid, w_qa, w_kva, cos, sin,
    f_part, attn, feed_chunks, collective_id,
):
    rows, width = tokens.shape
    rank = q_pre.shape[1]
    vmem = pl.BlockSpec(memory_space=pltpu.VMEM)
    anywhere = pl.BlockSpec(memory_space=pl.ANY)
    half, full = jnp.bfloat16, jnp.float32
    dma = pltpu.SemaphoreType.DMA
    share = (2 * width + rank + KVR) // n
    lines = -(-share // (32 * HEAD)) * 32
    plans = [
        Scatter(n, width // n, rank, False),
        Scatter(n, width // n, KVR + ROPE, False),
        Scatter(n, lines, HEAD, True),
    ]
    slots = pltpu.VMEM((2, rows // 4, width), full)
    chunked = (-1, CHUNK, width)
    grad_in, qa, kva, gains, layer_out = pl.pallas_call(
        functools.partial(down_tail_kernel, n, tp, plans, feed_chunks),
        out_shape=(
            jax.ShapeDtypeStruct((rows, width), full),
            *[jax.ShapeDtypeStruct((plan.rows, plan.columns), half) for plan in plans],
            jax.ShapeDtypeStruct((feed_chunks, CHUNK, width), half),
        ),
        in_specs=[vmem] * 12 + [anywhere] * 3,
        out_specs=(anywhere, vmem, vmem, vmem, vmem),
        scratch_shapes=[
            pltpu.VMEM((rows, rank), half),
            pltpu.VMEM((rows, KVR + ROPE), half),
            pltpu.VMEM((width, rows), half),
            pltpu.VMEM((rows, HEAD), full),
            pltpu.VMEM((1, width), full),
            pltpu.VMEM((1, rank), full),
            pltpu.VMEM((1, KVR), full),
            pltpu.VMEM((n * lines, HEAD), half),
            pltpu.VMEM((n * lines, HEAD), full),
            slots,
            dma((2,)),
            *[shape for plan in plans for shape in plan.scratch()],
            *feed_scratch(feed_chunks, width),
        ],
        compiler_params=pltpu.CompilerParams(
            vmem_limit_bytes=MIDDLE_VMEM, collective_id=collective_id, has_side_effects=True
        ),
        cost_estimate=pl.CostEstimate(
            flops=4 * rows * width * (rank + KVR + ROPE),
            bytes_accessed=40 * 1024 * 1024,
            transcendentals=rows,
        ),
        name=f"down_tail_{collective_id}",
    )(
        sum_q,
        sum_lat,
        q_pre,
        lat_raw,
        tokens,
        d_attn,
        gain_row,
        g_mid,
        w_qa,
        w_kva,
        cos,
        sin,
        *[array.reshape(chunked) for array in (f_part, tokens, attn)],
    )
    gains = gains.astype(full).reshape(-1)
    ends = [0]
    for size in (width, width, rank, KVR):
        ends.append(ends[-1] + size // n)
    own_gains = [gains[first:last] for first, last in zip(ends, ends[1:])]
    return grad_in, qa, kva, own_gains, layer_out.reshape(-1, width)


CHUNK = 16
BLOCK = 8 * CHUNK
LAG = 2
MIDDLE_VMEM = 63 * 1024 * 1024


def middle_kernel(
    n, lag, ob, tokens_in, cot_in, gain, w_out, w_gate, w_up, w_down,
    tt_to, d_to, f_to, act_to, dg_to, du_to, h_to, df_to,
    tt, d_out, f_out, act_out, dg_out, du_out, h_out, df_out,
    tokens, cot, own, up, wo, wg, wu, wd, d_acc, f_acc, w_sems, out_sems, *sems,
):
    line = LineSum(n, own, up, tt, sems, lag)
    width = tokens.shape[1]
    hidden = wg.shape[0]
    chunks, chunk = own.shape[:2]
    per_block = BLOCK // chunk
    blocks = chunks // per_block
    block_lag = -(-(per_block + line.land_lag) // per_block)
    tiles = [(c, min(c + 512, width)) for c in range(0, width, 512)]
    quarter = hidden // 4 // 128 * 128
    cuts = [0, quarter, 2 * quarter, 3 * quarter, hidden]
    loads = [
        pltpu.make_async_copy(source, target, w_sems.at[k])
        for k, (source, target) in enumerate(
            (
                (w_out, wo),
                (tokens_in, tokens),
                (cot_in, cot),
                (w_gate, wg),
                (w_up, wu),
                (w_down, wd),
            )
        )
    ]
    kept = ((d_out, d_to), (f_out, f_to), (act_out, act_to), (dg_out, dg_to), (du_out, du_to))
    kept += ((h_out, h_to), (df_out, df_to))

    def keep(b):
        rows = pl.ds(pl.multiple_of(b * BLOCK, BLOCK), BLOCK)
        copies = [
            pltpu.make_async_copy(source.at[rows, :], target.at[rows, :], out_sems.at[k, b])
            for k, (source, target) in enumerate(kept)
        ]
        some = pl.ds(b * per_block, per_block)
        return copies + [
            pltpu.make_async_copy(tt.at[some], tt_to.at[some], out_sems.at[len(kept), b])
        ]

    for load in loads:
        load.start()
    barrier = pltpu.get_barrier_semaphore()
    line.greet(barrier)
    line.wait_greetings(barrier, 0)

    def project(b, carry):
        rows = pl.ds(pl.multiple_of(b * BLOCK, BLOCK), BLOCK)
        for first, last in tiles:
            part = dot_nt(ob[rows, :], wo[first:last, :]).astype(jnp.bfloat16)
            for k in range(per_block):
                own[per_block * b + k, :, first:last] = part[k * chunk : (k + 1) * chunk, :]
        for k in range(per_block):
            line.leaf(per_block * b + k)
        return carry

    def normalize(b, part):
        for k in range(part * per_block // 2, (part + 1) * per_block // 2, 2):
            rows = pl.ds(pl.multiple_of(b * BLOCK + k * chunk, 2 * chunk), 2 * chunk)
            sums = jnp.concatenate([tt[b * per_block + k], tt[b * per_block + k + 1]], axis=0)
            middle = tokens[rows, :].astype(jnp.float32) + RESIDUAL_SCALE * sums.astype(jnp.float32)
            h_out[rows, :] = (middle * norm_scale(middle) * gain[:, width : 2 * width]).astype(jnp.bfloat16)

    def feed(b, i):
        rows = pl.ds(pl.multiple_of(b * BLOCK, BLOCK), BLOCK)
        first, last = cuts[i], cuts[i + 1]
        if i == 0:
            normalize(b, 0)
            normalize(b, 1)
            df_out[rows, :] = (RESIDUAL_SCALE * cot[rows, :].astype(jnp.float32)).astype(
                jnp.bfloat16
            )
        gate = dot_nt(h_out[rows, :], wg[first:last, :])
        upper = dot_nt(h_out[rows, :], wu[first:last, :])
        d_act = dot_nt(df_out[rows, :], wd[first:last, :])
        sig = jax.nn.sigmoid(gate)
        silu = gate * sig
        act_out[rows, first:last] = (silu * upper).astype(jnp.bfloat16)
        dg_out[rows, first:last] = (d_act * upper * sig * (1.0 + gate * (1.0 - sig))).astype(
            jnp.bfloat16
        )
        du_out[rows, first:last] = (d_act * silu).astype(jnp.bfloat16)

    def feed_back(b, i):
        rows = pl.ds(pl.multiple_of(b * BLOCK, BLOCK), BLOCK)
        first, last = cuts[i], cuts[i + 1]
        act, dg, du = (ref[rows, first:last] for ref in (act_out, dg_out, du_out))
        for lo, hi in tiles:
            d_part = dot_nn(dg, wg[first:last, lo:hi]) + dot_nn(du, wu[first:last, lo:hi])
            f_part = dot_nn(act, wd[first:last, lo:hi])
            if i:
                d_part = d_part + d_acc[:, lo:hi]
                f_part = f_part + f_acc[:, lo:hi]
            if i < 3:
                d_acc[:, lo:hi] = d_part
                f_acc[:, lo:hi] = f_part
            else:
                d_out[rows, lo:hi] = d_part.astype(jnp.bfloat16)
                f_out[rows, lo:hi] = f_part.astype(jnp.bfloat16)

    loads[0].wait()
    lax.fori_loop(0, blocks, project, 0)

    def outer(o, carry):
        b = o - block_lag

        @pl.when(b == 0)
        def _():
            for load in loads[1:]:
                load.wait()

        share = per_block // 8
        for i in range(4):
            for step, work in enumerate((feed, feed_back)):

                @pl.when(o * per_block < line.ticks)
                def _(at=(2 * i + step) * share):
                    for k in range(share):
                        line.duty(o * per_block + at + k)

                @pl.when(b >= 0)
                def _(i=i, work=work):
                    work(b, i)

        @pl.when(b >= 0)
        def _():
            for copy in keep(b):
                copy.start()

        return carry

    lax.fori_loop(0, blocks + block_lag, outer, 0)
    line.drain()

    def finish(b, carry):
        for copy in keep(b):
            copy.wait()
        return carry

    lax.fori_loop(0, blocks, finish, 0)


def middle_layer(n, ob, tokens, cot, gains, w_out, w_gate, w_up, w_down, collective_id):
    rows, width = tokens.shape
    hidden = w_gate.shape[0]
    chunks = rows // CHUNK
    vmem = pl.BlockSpec(memory_space=pltpu.VMEM)
    anywhere = pl.BlockSpec(memory_space=pl.ANY)
    half = jnp.bfloat16
    dma = pltpu.SemaphoreType.DMA
    attn, *rest = pl.pallas_call(
        functools.partial(middle_kernel, n, LAG),
        out_shape=(
            jax.ShapeDtypeStruct((chunks, CHUNK, width), half),
            jax.ShapeDtypeStruct((rows, width), half),
            jax.ShapeDtypeStruct((rows, width), half),
            jax.ShapeDtypeStruct((rows, hidden), half),
            jax.ShapeDtypeStruct((rows, hidden), half),
            jax.ShapeDtypeStruct((rows, hidden), half),
            jax.ShapeDtypeStruct((rows, width), half),
            jax.ShapeDtypeStruct((rows, width), half),
        ),
        in_specs=[vmem, anywhere, anywhere, vmem] + [anywhere] * 4,
        out_specs=(anywhere,) * 8,
        scratch_shapes=[
            pltpu.VMEM((chunks, CHUNK, width), half),
            pltpu.VMEM((rows, width), half),
            pltpu.VMEM((rows, width), half),
            pltpu.VMEM((rows, hidden), half),
            pltpu.VMEM((rows, hidden), half),
            pltpu.VMEM((rows, hidden), half),
            pltpu.VMEM((rows, width), half),
            pltpu.VMEM((rows, width), half),
            pltpu.VMEM((rows, width), half),
            pltpu.VMEM((rows, width), half),
            pltpu.VMEM((chunks, CHUNK, width), half),
            pltpu.VMEM((chunks, CHUNK, width), half),
            pltpu.VMEM(w_out.shape, half),
            pltpu.VMEM(w_gate.shape, half),
            pltpu.VMEM(w_up.shape, half),
            pltpu.VMEM(w_down.shape, half),
            pltpu.VMEM((BLOCK, width), jnp.float32),
            pltpu.VMEM((BLOCK, width), jnp.float32),
            dma((6,)),
            dma((8, rows // BLOCK)),
            *line_sems(chunks),
        ],
        compiler_params=pltpu.CompilerParams(
            vmem_limit_bytes=MIDDLE_VMEM, collective_id=collective_id, has_side_effects=True
        ),
        cost_estimate=pl.CostEstimate(
            flops=2 * rows * width * (6 * hidden + ob.shape[1]),
            bytes_accessed=64 * 1024 * 1024,
            transcendentals=rows * hidden,
        ),
        name=f"middle_layer_{collective_id}",
    )(ob, tokens, cot, gains, w_out, w_gate, w_up, w_down)
    return attn.reshape(rows, width), *rest


def norm_scale(values):
    return lax.rsqrt(jnp.mean(values * values, axis=-1, keepdims=True) + EPSILON)


def norm_back(incoming, values, inv_rms, gain_vec):
    weighted = incoming * gain_vec
    mean = jnp.mean(weighted * values, axis=-1, keepdims=True)
    d_values = inv_rms * weighted - values * (inv_rms * inv_rms * inv_rms) * mean
    return d_values, jnp.sum(incoming * values * inv_rms, axis=0, keepdims=True)


def rope_tile(tile, cos, sin, lane):
    left = pltpu.roll(tile, HEAD - ROPE // 2, 1)
    right = pltpu.roll(tile, ROPE // 2, 1)
    swapped = jnp.where(lane < ROPE // 2, -left, right)
    return jnp.where(lane < ROPE, tile * cos + swapped * sin, 0.0)


def rope_tile_back(tile, cos, sin, lane):
    shifted = tile * sin
    left = pltpu.roll(shifted, HEAD - ROPE // 2, 1)
    right = pltpu.roll(shifted, ROPE // 2, 1)
    swapped = jnp.where(lane < ROPE // 2, left, -right)
    return jnp.where(lane < ROPE, tile * cos + swapped, 0.0)


def split_gains(gains, width, rank):
    ends = (0, width, 2 * width, 2 * width + rank, 2 * width + rank + KVR)
    return [gains[:, first:last] for first, last in zip(ends, ends[1:])]


def head_kernel(
    n, block_map, lengths, tokens, gains, rates, w_qa, w_kva, w_qb,
    out, q_latent, q_pre, lat_raw, cos, sin, qx, qt,
    own, normed, w_rope, flat, local_sem, step_sends, step_lands, core_sends, core_lands,
):
    gain_in, _, gain_q, gain_kv = split_gains(gains, tokens.shape[1], w_qa.shape[1])
    heads = qx.shape[1]
    count = n.bit_length() - 1
    me = lax.axis_index("ctx")
    rows = own.shape[0]
    half = rows // 2
    block = rows // 4
    barrier = pltpu.get_barrier_semaphore()
    for bit in range(count):
        pl.semaphore_signal(barrier, inc=1, device_id={"ctx": me ^ (1 << bit)}, device_id_type=MESH)
    orders = (tuple(range(1, count)), tuple(range(count - 1, 0, -1)))
    lane = lax.broadcasted_iota(jnp.int32, (block, HEAD), 1)
    w_rope[...] = jnp.zeros(w_rope.shape, jnp.bfloat16)
    w_rope[:ROPE, :] = w_kva[KVR : KVR + ROPE, :]

    starts = starts_of(lengths)
    places = lax.broadcasted_iota(jnp.int32, (half, HEAD), 0)
    lanes = lax.broadcasted_iota(jnp.int32, (half, HEAD), 1)
    for j in range(2):
        at = pl.ds(j * half, half)
        place = block_map[j, me] * half + places
        angles = (place - begin_of(place, starts)).astype(jnp.float32) * rates[...]
        cos[at, :] = jnp.where(lanes < ROPE, jnp.cos(angles), 0.0)
        sin[at, :] = jnp.where(lanes < ROPE, jnp.sin(angles), 0.0)

    def latents(k, carry):
        at = pl.ds(pl.multiple_of(k * block, block), block)
        values = tokens[at, :].astype(jnp.float32)
        normed[at, :] = (values * norm_scale(values) * gain_in).astype(jnp.bfloat16)
        raw = dot_nt(normed[at, :], w_kva[:KVR, :])
        lat_raw[at, :] = raw
        own[at, :KVR] = (raw * norm_scale(raw) * gain_kv).astype(jnp.bfloat16)
        rope = rope_tile(dot_nt(normed[at, :], w_rope[...]), cos[at, :], sin[at, :], lane)
        own[at, KVR:] = rope[:, :ROPE].astype(jnp.bfloat16)
        return carry

    lax.fori_loop(0, 4, latents, 0)
    pl.semaphore_wait(barrier, count)
    local = pltpu.make_async_copy(own, out.at[me], local_sem)
    local.start()

    def chip_copy(part, step, slot, block, first):
        at = pl.ds(part * half, half)
        return pltpu.make_async_remote_copy(
            src_ref=own.at[at, :] if first else out.at[block, at, :],
            dst_ref=out.at[block, at, :],
            send_sem=step_sends.at[part, step, slot],
            recv_sem=step_lands.at[part, step, slot],
            device_id={"ctx": me ^ (1 << orders[part][step])},
            device_id_type=MESH,
        )

    def core_copy(block, slot, first):
        return pltpu.make_async_remote_copy(
            src_ref=own if first else out.at[block],
            dst_ref=out.at[block],
            send_sem=core_sends.at[slot],
            recv_sem=core_lands.at[slot],
            device_id={"ctx": me ^ 1},
            device_id_type=MESH,
        )

    def query(k, carry):
        at = pl.ds(pl.multiple_of(k * block, block), block)
        pre = dot_nn(normed[at, :], w_qa[...])
        q_pre[at, :] = pre
        q_latent[at, :] = (pre * norm_scale(pre) * gain_q).astype(jnp.bfloat16)
        return carry

    def queries(j):
        here = pl.ds(j * half, half)
        cos_j, sin_j = cos[here, :], sin[here, :]
        width = heads * (NOPE + ROPE)
        for at in range(0, width, WIDE):
            end = min(at + WIDE, width)
            flat[:, at:end] = dot_nt(q_latent[here, :], w_qb[at:end, :])
        for h in range(heads):
            at, shift = head_window(h)
            own_part = pltpu.roll(flat[:, at : at + WIDE], (WIDE - shift) % WIDE, 1)[:, :HEAD]
            nope = jnp.where(lanes < NOPE, own_part, 0.0)
            rope = rope_tile(pltpu.roll(own_part, NOPE, 1), cos_j, sin_j, lanes)
            qx[j, h, :, :HEAD] = nope.astype(jnp.bfloat16)
            qx[j, h, :, HEAD:] = rope.astype(jnp.bfloat16)
            qt[j, h, :NOPE, :] = nope.T[:NOPE, :].astype(jnp.bfloat16)
            qt[j, h, NOPE:, :] = rope.T[:ROPE, :].astype(jnp.bfloat16)

    started = []
    for step in range(count - 1):
        for part, order in enumerate(orders):
            for slot in range(1 << step):
                flips = 0
                for at in range(step):
                    flips |= ((slot >> at) & 1) << order[at]
                copy = chip_copy(part, step, slot, me ^ flips, slot == 0)
                copy.start()
                started.append(copy)
        if step == 0:
            core_copy(me, 0, True).start()
        lax.fori_loop(min(2 * step, 4), min(2 * step + 2, 4) if step < count - 2 else 4, query, 0)
        if step == count - 2:
            queries(0)
        for part, order in enumerate(orders):
            for slot in range(1 << step):
                chip_copy(part, step, slot, me, slot == 0).wait_recv()
    for chip in range(1, n // 2):
        core_copy(me ^ (2 * chip), chip, False).start()
    queries(1)
    for chip in range(n // 2):
        core_copy(me, chip, chip == 0).wait_recv()
    for copy in started:
        copy.wait_send()
    for chip in range(n // 2):
        core_copy(me, chip, chip == 0).wait_send()
    local.wait()


def head_layer(n, block_map, lengths, tokens, gains, w_qa, w_kva, w_qb, collective_id):
    rows, width = tokens.shape
    rank = w_qa.shape[1]
    count = n.bit_length() - 1
    vmem = pl.BlockSpec(memory_space=pltpu.VMEM)
    slots = max(n // 4, 1)
    dma = pltpu.SemaphoreType.DMA
    smem = pl.BlockSpec(memory_space=pltpu.SMEM)
    heads = w_qb.shape[0] // (NOPE + ROPE)
    pairs = (2, heads)
    lane = np.arange(HEAD)
    rates = ROPE_BASE ** (-2.0 * (lane % (ROPE // 2)) / ROPE)
    gathered, *rest = pl.pallas_call(
        functools.partial(head_kernel, n),
        out_shape=(
            jax.ShapeDtypeStruct((n, rows, KVR + ROPE), jnp.bfloat16),
            jax.ShapeDtypeStruct((rows, rank), jnp.bfloat16),
            jax.ShapeDtypeStruct((rows, rank), jnp.float32),
            jax.ShapeDtypeStruct((rows, KVR), jnp.float32),
            jax.ShapeDtypeStruct((rows, HEAD), jnp.float32),
            jax.ShapeDtypeStruct((rows, HEAD), jnp.float32),
            jax.ShapeDtypeStruct((*pairs, rows // 2, WIDE), jnp.bfloat16),
            jax.ShapeDtypeStruct((*pairs, NOPE + ROPE, rows // 2), jnp.bfloat16),
        ),
        in_specs=[smem] * 2 + [vmem] * 6,
        out_specs=(vmem,) * 8,
        scratch_shapes=[
            pltpu.VMEM((rows, KVR + ROPE), jnp.bfloat16),
            pltpu.VMEM((rows, width), jnp.bfloat16),
            pltpu.VMEM((HEAD, width), jnp.bfloat16),
            pltpu.VMEM((rows // 2, window_columns(heads)), jnp.float32),
            dma,
            dma((2, count - 1, slots)),
            dma((2, count - 1, slots)),
            dma((n // 2,)),
            dma((n // 2,)),
        ],
        compiler_params=pltpu.CompilerParams(
            vmem_limit_bytes=VMEM_LIMIT, collective_id=collective_id, has_side_effects=True
        ),
        cost_estimate=pl.CostEstimate(
            flops=2 * rows * width * (rank + KVR + ROPE),
            bytes_accessed=24 * 1024 * 1024,
            transcendentals=rows,
        ),
        name=f"head_layer_{collective_id}",
    )(
        block_map,
        lengths,
        tokens,
        gains,
        jnp.asarray(rates.astype(np.float32).reshape(1, -1)),
        w_qa,
        w_kva,
        w_qb,
    )
    return gathered.reshape(n * rows, -1), *rest


def on_device(
    tokens_in,
    w_qa,
    w_kva,
    w_qb,
    w_kvb,
    w_out,
    w_gate,
    w_up,
    w_down,
    gain_in,
    gain_q,
    gain_kv,
    gain_mid,
    cotangent,
    block_map,
    doc_lengths,
):
    devices = lax.axis_size("ctx")
    block_map = block_map.T
    gains = jnp.concatenate([gain_in, gain_mid, gain_q, gain_kv]).reshape(1, -1)
    latents, q_latent, q_latent_pre, latent_raw, cosine, sine, queries, queries_t = head_layer(
        devices, block_map, doc_lengths, tokens_in, gains, w_qa, w_kva.T, w_qb.T, 0
    )
    attn_f, heads_out, log_totals = attention_forward(
        block_map, doc_lengths, queries, latents, w_kvb
    )
    attention, d_part, feed_part, activation, d_gate, d_up, normed_mid, d_feed = middle_layer(
        lax.axis_size("tp"), heads_out, tokens_in, cotangent, gains, w_out, w_gate.T, w_up.T,
        w_down.T, 5,
    )
    gw_gate, gw_up, d_attention, d_heads, d_gain_mid = gate_up_grads(
        devices, lax.axis_size("tp"), normed_mid, d_gate, d_up, d_part, tokens_in, attention,
        cotangent, gains, w_out, 1,
    )
    d_query_pre, d_latents, gw_kvb = attention_backward(
        block_map, doc_lengths, queries, queries_t, log_totals, attn_f, d_heads, latents, w_kvb,
        cosine, sine,
    )
    chunks = tokens_in.shape[0] // CHUNK
    sum_q, sum_lat, gw_down, gw_out, gw_qb, gw_kvb, out_first = up_tail(
        devices, lax.axis_size("tp"), d_latents, d_query_pre, w_qb.T, gw_kvb, d_attention, heads_out,
        q_latent, d_feed, activation, feed_part, tokens_in, attention, chunks // 2, 2,
    )
    grad_in, gw_qa, gw_kva, own_gains, out_second = down_tail(
        devices, lax.axis_size("tp"), sum_q, sum_lat, q_latent_pre, latent_raw, tokens_in,
        d_attention, gains, d_gain_mid, w_qa, w_kva.T, cosine, sine, feed_part, attention,
        chunks - chunks // 2, 3,
    )
    out = jnp.concatenate([out_first, out_second], axis=0)
    grads = (gw_qa, gw_kva, gw_qb, gw_kvb, gw_out, gw_gate, gw_up, gw_down)
    return (
        out,
        grad_in,
        *[grad.astype(jnp.float32) for grad in grads],
        own_gains[0],
        own_gains[2],
        own_gains[3],
        own_gains[1],
    )


def solution(mesh):
    return jax.shard_map(
        on_device,
        mesh=mesh,
        in_specs=(
            P("ctx", None),
            P(),
            P(),
            P(None, "tp"),
            P(None, "tp"),
            P(None, "tp"),
            P(None, "tp"),
            P(None, "tp"),
            P(None, "tp"),
            P(),
            P(),
            P(),
            P(),
            P("ctx", None),
            P(),
            P(),
        ),
        out_specs=(
            P("ctx", None),
            P("ctx", None),
            P("ctx", None),
            P("ctx", None),
            P("ctx", "tp"),
            P("ctx", "tp"),
            P("ctx", "tp"),
            P("ctx", "tp"),
            P("ctx", "tp"),
            P("ctx", "tp"),
            P("ctx"),
            P("ctx"),
            P("ctx"),
            P("ctx"),
        ),
        check_vma=False,
    )
```

profile of v0, /device:TPU:0, one launch (start us, length us, event | category | flops | bytes accessed | tf_op | source)
XLA Modules:
  0.0 497.7 jit_solution(8382057710888175992)
XLA Ops:
  0.6 1.4 pad_maximum_fusion.1
  2.0 33.5 %head_layer_0.1 = (bf16[8,512,288]{2,1,0:T(8,128)(2,1)}, bf16[512,768]{1,0:T(8,128)(2,1)}, f32[512,768]{1,0:T(8,128)}, f32[512,256]{1,0:T(8,128)}, f32[512,128]{...) custom-call(s32[2,8]{1,0:T(2,128)} %bitcast.41, s32[4]{0:T(128)} %lengths.5, ...), custom_call_target="tpu_custom_call" | custom-call | flops 2768240640 | bytes 25165824 | tf_op jit(solution)/shard_map/head_layer_0/pallas_call | solution.py:1672
  35.5 30.0 %attention_forward.1 = (f32[512,640]{1,0:T(8,128)}, bf16[512,640]{1,0:T(8,128)(2,1)}, f32[2,16,256]{2,1,0:T(8,128)}) custom-call(s32[2,8]{1,0:T(2,128)} %bitcast.42, s32[4]{0:T(128)} %lengths.5, bf16[2,10,256,256]{3,2,1,0:T(8,128)(2,1)} %get-tuple-element.53.qx, bf16[4096,288]{1,0:T(8,128)(2,1)} %bitcast.44, bf16[256,1280]{1,0:T(8,128)(2,1)} %wkvb.3), custom_call_target="tpu_custom_call" | custom-call | flops 10737418240 | bytes 16777216 | tf_op jit(solution)/shard_map/attention_forward/pallas_call | solution.py:208
  65.5 97.4 %middle_layer_5.1 = (bf16[32,16,2560]{2,1,0:T(8,128)(2,1)}, bf16[512,2560]{1,0:T(8,128)(2,1)}, bf16[512,2560]{1,0:T(8,128)(2,1)}, bf16[512,1600]{1,0:T(8,128)(2,...) custom-call(bf16[512,640]{1,0:T(8,128)(2,1)} %get-tuple-element.58.o, ...), custom_call_target="tpu_custom_call" | custom-call | flops 26843545600 | bytes 67108864 | tf_op jit(solution)/shard_map/middle_layer_5/pallas_call | solution.py:1458
  162.9 89.3 %gate_up_grads_1.1 = (bf16[320,1600]{1,0:T(8,128)(2,1)}, bf16[320,1600]{1,0:T(8,128)(2,1)}, bf16[512,2560]{1,0:T(8,128)(2,1)}, bf16[512,640]{1,0:T(8,128)(2,1)}, f32[1,2560]{1,0:T(1,128)}) custom-call(bf16[512,2560]{1,0:T(8,128)(2,1)} %get-tuple-element.59.normed, bf16[512,1600]{1,0:T(8,128)(2,1)} %get-tuple-element.60.d_gate, ...), custom_call_target="tpu_custom_call" | custom-call | flops 10066329600 | bytes 29360128 | tf_op jit(solution)/shard_map/gate_up_grads_1/pallas_call | solution.py:880
  252.2 55.0 %attention_backward.1 = (bf16[512,960]{1,0:T(8,128)(2,1)}, bf16[4096,288]{1,0:T(8,128)(2,1)}, bf16[256,1280]{1,0:T(8,128)(2,1)}) custom-call(s32[2,8]{1,0:T(2,128)} %bitcast.43, s32[4]{0:T(128)} %lengths.5, bf16[2,10,256,256]{3,2,1,0:T(8,128)(2,1)} %get-tuple-element.53.qx, bf16[2,10,96,256]{3,2,1,0:T(8,128)(2,1)} %get-tuple-element.54.qt, ...), custom_call_target="tpu_custom_call" | custom-call | flops 21474836480 | bytes 25165824 | tf_op jit(solution)/shard_map/attention_backward/pallas_call | solution.py:403
  307.2 103.7 %up_tail_2.1 = (bf16[8,64,768]{2,1,0:T(8,128)(2,1)}, bf16[8,64,288]{2,1,0:T(8,128)(2,1)}, bf16[320,1600]{1,0:T(8,128)(2,1)}, bf16[320,640]{1,0:T(8,128)(2,1)}, b...) custom-call(bf16[4096,288]{1,0:T(8,128)(2,1)} %get-tuple-element.67.d_lat, ...), custom_call_target="tpu_custom_call" | custom-call | flops 7381975040 | bytes 33554432 | tf_op jit(solution)/shard_map/up_tail_2/pallas_call | solution.py:1061
  410.9 70.0 %down_tail_3.1 = (f32[512,2560]{1,0:T(8,128)}, bf16[320,768]{1,0:T(8,128)(2,1)}, bf16[320,288]{1,0:T(8,128)(2,1)}, bf16[32,128]{1,0:T(8,128)(2,1)}, bf16[16,16,2560]{2,1,0:T(8,128)(2,1)}) custom-call(bf16[512,768]{1,0:T(8,128)(2,1)} %bitcast.30, bf16[512,288]{1,0:T(8,128)(2,1)} %bitcast.31, f32[512,768]{1,0:T(8,128)} %get-tuple-element.78.q_pre, ...), custom_call_target="tpu_custom_call" | custom-call | flops 5536481280 | bytes 41943040 | tf_op jit(solution)/shard_map/down_tail_3/pallas_call | solution.py:1243
  480.8 0.0 copy-start.8
  480.9 0.0 copy-start.7
  480.9 0.0 copy-start.6
  480.9 0.0 copy-start.5
  480.9 0.0 copy-start.4
  480.9 3.5 pad_maximum_fusion
  484.3 0.0 copy-done.8
  484.4 0.6 slice.18
  484.9 0.5 slice.17
  485.5 0.7 fusion
  486.1 0.0 copy-done.7
  486.1 0.7 convert_element_type.28
  486.8 0.0 copy-done.6
  486.8 0.8 convert_element_type.27
  487.6 0.0 copy-done.5
  487.6 0.9 copy.31
  488.5 0.0 copy-done.4
  488.5 0.9 convert_element_type.29
  489.4 0.0 copy-done.3
  489.4 1.0 convert_element_type.25
  490.5 1.5 convert_element_type.32
  491.9 1.5 convert_element_type.30
  493.4 1.5 convert_element_type.31
  494.9 2.4 copy.33
  (13 shorter events, 0.0 us)
Async XLA Ops:
  480.8 3.5 copy-start.8
  480.9 5.3 %copy-start.7 = (bf16[32,1280]{1,0:T(8,128)(2,1)S(1)}, bf16[32,1280]{1,0:T(8,128)(2,1)}, u32[]{:S(2)}) copy-start(bf16[32,1280]{1,0:T(8,128)(2,1)} %get-tuple-element.86) | copy-start | bytes 245764
  480.9 5.9 %copy-start.6 = (bf16[96,960]{1,0:T(8,128)(2,1)S(1)}, bf16[96,960]{1,0:T(8,128)(2,1)}, u32[]{:S(2)}) copy-start(bf16[96,960]{1,0:T(8,128)(2,1)} %get-tuple-element.85) | copy-start | bytes 552964
  480.9 6.7 %copy-start.5 = (bf16[320,288]{1,0:T(8,128)(2,1)S(1)}, bf16[320,288]{1,0:T(8,128)(2,1)}, u32[]{:S(2)}) copy-start(bf16[320,288]{1,0:T(8,128)(2,1)} %get-tuple-element.84) | copy-start | bytes 552964
  480.9 7.6 %copy-start.4 = (bf16[320,640]{1,0:T(8,128)(2,1)S(1)}, bf16[320,640]{1,0:T(8,128)(2,1)}, u32[]{:S(2)}) copy-start(bf16[320,640]{1,0:T(8,128)(2,1)} %get-tuple-element.87) | copy-start | bytes 1228804
  484.4 5.1 %copy-start.3 = (bf16[320,768]{1,0:T(8,128)(2,1)S(1)}, bf16[320,768]{1,0:T(8,128)(2,1)}, u32[]{:S(2)}) copy-start(bf16[320,768]{1,0:T(8,128)(2,1)} %get-tuple-element.83) | copy-start | bytes 1474564
  484.4 6.1 %copy-start.2 = (bf16[320,1600]{1,0:T(8,128)(2,1)S(1)}, bf16[320,1600]{1,0:T(8,128)(2,1)}, u32[]{:S(2)}) copy-start(bf16[320,1600]{1,0:T(8,128)(2,1)} %get-tuple-element.90) | copy-start | bytes 3072004
  487.6 7.3 %slice-start = ((s8[5242880]{0:T(1024)(128)(4,1)}), s8[1048576]{0:T(1024)(128)(4,1)S(1)}, s32[]{:S(2)}) async-start(s8[5242880]{0:T(1024)(128)(4,1)} %bitcast.21), calls=%async_computation | async-start | bytes 2097152
  489.4 2.5 copy-start.1
  490.5 2.9 copy-start
  490.5 4.4 slice-start.1
where the time goes:
time: 505 us; the launch traced here: 498 us
  Pallas kernels  479 us (95%)
  other arithmetic  12.6 us (2%)
  local copies, waits for them, and re-layouts  5.06 us (1%)
    pallas_call x1, Pallas kernels, up_tail(): pl.pallas_call(functools.partial(up_tail_kernel, n, tp, plans, feed_chunk...  104 us
    pallas_call x1, Pallas kernels, middle_layer(): pl.pallas_call(functools.partial(middle_kernel, n, LAG), out_shape=(jax.S...  97.4 us
    pallas_call x1, Pallas kernels, gate_up_grads(): pl.pallas_call(functools.partial(gate_up_kernel, n, tp, plans), out_shape...  89.3 us
    pallas_call x1, Pallas kernels, down_tail(): pl.pallas_call(functools.partial(down_tail_kernel, n, tp, plans, feed_chu...  70 us
    pallas_call x1, Pallas kernels, attention_backward(): pl.pallas_call(functools.partial(backward_kernel, blocks, heads), out_sha...  55 us
    pallas_call x1, Pallas kernels, head_layer(): pl.pallas_call(functools.partial(head_kernel, n), out_shape=(jax.ShapeDty...  33.5 us
    pallas_call x1, Pallas kernels, attention_forward(): pl.pallas_call(functools.partial(forward_kernel, blocks, heads), out_shap...  30 us

commit v1 on v0

--- a/solution.py
+++ b/solution.py
@@ -922,7 +922,7 @@
             pltpu.make_async_copy(source.at[some], target, sems.at[k])
             for k, (source, target) in enumerate(pairs)
         ]
-        self.line = LineSum(tp, own, landing, sums, take(5), LAG)
+        self.line = LineSum(tp, own, landing, sums, take(5), FEED_LAG)
         self.ticks = self.line.ticks
 
     def load(self):
@@ -960,6 +960,7 @@
 
 
 TAIL_CHUNK = 64
+FEED_LAG = 4
 
 
 def up_tail_kernel(
@@ -968,7 +969,7 @@
 ):
     take = taker(refs)
     own_q, land_q, own_lat, land_lat, d_attn_t, q_latent_t, d_feed_t = take(7)
-    line_q = LineSum(tp, own_q, land_q, sum_q, take(5), LAG)
+    line_q = LineSum(tp, own_q, land_q, sum_q, take(5), LAG + 1)
     line_lat = LineSum(tp, own_lat, land_lat, sum_lat, take(5), LAG)
     feed = FeedSum(tp, take, 0, feed_chunks, f_part, tokens, attn, layer_out)
     feed.load()
@@ -1013,25 +1014,34 @@
     down.start_step(0)
     feed.begin()
     chips = n // 2
+
+    def both(line, line_first, feed_first):
+        def also(chip):
+            if line is not None:
+                line.duty(line_first + chip)
+            feed.duty(feed_first + chip)
+
+        return also
+
     turn(d_attn, d_attn_t)
-    out.start_core(line_q.duty)
-    out.finish_core(lambda chip: line_q.duty(chips + chip))
+    out.start_core(both(line_q, 0, 0))
+    out.finish_core(both(line_q, chips, chips))
     out.start_step(0)
-    kvb.start_core()
+    kvb.start_core(both(None, 0, 2 * chips))
     turn(q_latent, q_latent_t)
-    qb.start_core(lambda chip: line_q.duty(2 * chips + chip))
-    kvb.finish_core()
+    qb.start_core(both(line_q, 2 * chips, 3 * chips))
+    kvb.finish_core(both(line_lat, 0, 4 * chips))
     kvb.start_step(0)
-    qb.finish_core(line_lat.duty)
+    qb.finish_core(both(line_lat, chips, 5 * chips))
     qb.start_step(0)
     steps = [(item, step) for step in range(lat.count - 1) for item in (down, out, kvb, qb)]
     q_share = spread(len(steps), line_q.ticks - 3 * chips)
-    lat_share = spread(len(steps), line_lat.ticks - chips)
-    feed_share = spread(len(steps), feed.ticks)
+    lat_share = spread(len(steps), line_lat.ticks - 2 * chips)
+    feed_share = spread(len(steps), feed.ticks - 6 * chips)
     for (item, step), (a, b), (c, d), (e, f) in zip(steps, q_share, lat_share, feed_share):
         line_q.pump(3 * chips + a, 3 * chips + b)
-        line_lat.pump(chips + c, chips + d)
-        feed.pump(e, f)
+        line_lat.pump(2 * chips + c, 2 * chips + d)
+        feed.pump(6 * chips + e, 6 * chips + f)
         item.finish_step(step)
     for item in (*plans, line_q, line_lat, feed.line):
         item.drain()
@@ -1145,6 +1155,7 @@
         ref[...] = jnp.zeros(ref.shape, jnp.float32)
 
     def norms(k, carry):
+        feed.duty(k)
         at = rows_of(k)
         pre = q_pre[at, :]
         d_pre, terms = norm_back(
@@ -1172,13 +1183,14 @@
 
     lax.fori_loop(0, 4, norms, 0)
     chips = n // 2
-    qa.start_core()
-    kva.start_core()
-    qa.finish_core()
+    qa.start_core(lambda chip: feed.duty(4 + chip))
+    qa.finish_core(lambda chip: feed.duty(4 + chips + chip))
     qa.start_step(0)
-    kva.finish_core(feed.duty)
+    kva.start_core(lambda chip: feed.duty(4 + 2 * chips + chip))
+    kva.finish_core(lambda chip: feed.duty(4 + 3 * chips + chip))
     kva.start_step(0)
-    shares = [(chips + a, chips + b) for a, b in spread(4 + 3, feed.ticks - chips)]
+    done = 4 + 4 * chips
+    shares = [(done + a, done + b) for a, b in spread(4 + 3, max(feed.ticks - done, 0))]
     for k in range(4):
         at = pl.ds(k * block, block)
         feed.pump(*shares[k])
@@ -1756,14 +1768,15 @@
         cosine, sine,
     )
     chunks = tokens_in.shape[0] // CHUNK
+    first_chunks = 3 * chunks // 4
     sum_q, sum_lat, gw_down, gw_out, gw_qb, gw_kvb, out_first = up_tail(
         devices, lax.axis_size("tp"), d_latents, d_query_pre, w_qb.T, gw_kvb, d_attention, heads_out,
-        q_latent, d_feed, activation, feed_part, tokens_in, attention, chunks // 2, 2,
+        q_latent, d_feed, activation, feed_part, tokens_in, attention, first_chunks, 2,
     )
     grad_in, gw_qa, gw_kva, own_gains, out_second = down_tail(
         devices, lax.axis_size("tp"), sum_q, sum_lat, q_latent_pre, latent_raw, tokens_in,
         d_attention, gains, d_gain_mid, w_qa, w_kva.T, cosine, sine, feed_part, attention,
-        chunks - chunks // 2, 3,
+        chunks - first_chunks, 3,
     )
     out = jnp.concatenate([out_first, out_second], axis=0)
     grads = (gw_qa, gw_kva, gw_qb, gw_kvb, gw_out, gw_gate, gw_up, gw_down)

time: 505 us -> 513 us (1.016); the launches traced: 498 us -> 511 us
  Pallas kernels: 479 us -> 492 us
    pallas_call x1, Pallas kernels: 104 us -> 148 us  [up_tail(): pl.pallas_call(functools.partial(up_tail_kernel, n, tp, plans, feed_chunk...]
    pallas_call x1, Pallas kernels: 55 us -> 28.8 us  [attention_backward(): pl.pallas_call(functools.partial(backward_kernel, blocks, heads), out_sha...]
    pallas_call x1, Pallas kernels: 89.3 us -> 109 us  [gate_up_grads(): pl.pallas_call(functools.partial(gate_up_kernel, n, tp, plans), out_shape...]
    pallas_call x1, Pallas kernels: 30 us -> 13.9 us  [attention_forward(): pl.pallas_call(functools.partial(forward_kernel, blocks, heads), out_shap...]
    pallas_call x1, Pallas kernels: 70 us -> 61.9 us  [down_tail(): pl.pallas_call(functools.partial(down_tail_kernel, n, tp, plans, feed_chu...]
where the time goes in v1:
time: 513 us; the launch traced here: 511 us
  Pallas kernels  492 us (96%)
  other arithmetic  12.7 us (2%)
    pallas_call x1, Pallas kernels, up_tail(): pl.pallas_call(functools.partial(up_tail_kernel, n, tp, plans, feed_chunk...  148 us
    pallas_call x1, Pallas kernels, gate_up_grads(): pl.pallas_call(functools.partial(gate_up_kernel, n, tp, plans), out_shape...  109 us
    pallas_call x1, Pallas kernels, middle_layer(): pl.pallas_call(functools.partial(middle_kernel, n, LAG), out_shape=(jax.S...  97.5 us
    pallas_call x1, Pallas kernels, down_tail(): pl.pallas_call(functools.partial(down_tail_kernel, n, tp, plans, feed_chu...  61.9 us
    pallas_call x1, Pallas kernels, head_layer(): pl.pallas_call(functools.partial(head_kernel, n), out_shape=(jax.ShapeDty...  33.5 us
    pallas_call x1, Pallas kernels, attention_backward(): pl.pallas_call(functools.partial(backward_kernel, blocks, heads), out_sha...  28.8 us
    pallas_call x1, Pallas kernels, attention_forward(): pl.pallas_call(functools.partial(forward_kernel, blocks, heads), out_shap...  13.9 us

profile of v1, /device:TPU:0, one launch (start us, length us, event | category | flops | bytes accessed | tf_op | source)
XLA Modules:
  0.0 510.9 jit_solution(6178390208461545249)
XLA Ops:
  0.6 1.4 pad_maximum_fusion.1
  2.0 33.5 %head_layer_0.1 = (bf16[8,512,288]{2,1,0:T(8,128)(2,1)}, bf16[512,768]{1,0:T(8,128)(2,1)}, f32[512,768]{1,0:T(8,128)}, f32[512,256]{1,0:T(8,128)}, f32[512,128]{...) custom-call(s32[2,8]{1,0:T(2,128)} %bitcast.41, s32[4]{0:T(128)} %lengths.5, ...), custom_call_target="tpu_custom_call" | custom-call | flops 2768240640 | bytes 25165824 | tf_op jit(solution)/shard_map/head_layer_0/pallas_call | solution.py:1684
  35.5 13.9 %attention_forward.1 = (f32[512,640]{1,0:T(8,128)}, bf16[512,640]{1,0:T(8,128)(2,1)}, f32[2,16,256]{2,1,0:T(8,128)}) custom-call(s32[2,8]{1,0:T(2,128)} %bitcast.42, s32[4]{0:T(128)} %lengths.5, bf16[2,10,256,256]{3,2,1,0:T(8,128)(2,1)} %get-tuple-element.53.qx, bf16[4096,288]{1,0:T(8,128)(2,1)} %bitcast.44, bf16[256,1280]{1,0:T(8,128)(2,1)} %wkvb.3), custom_call_target="tpu_custom_call" | custom-call | flops 10737418240 | bytes 16777216 | tf_op jit(solution)/shard_map/attention_forward/pallas_call | solution.py:208
  49.5 97.5 %middle_layer_5.1 = (bf16[32,16,2560]{2,1,0:T(8,128)(2,1)}, bf16[512,2560]{1,0:T(8,128)(2,1)}, bf16[512,2560]{1,0:T(8,128)(2,1)}, bf16[512,1600]{1,0:T(8,128)(2,...) custom-call(bf16[512,640]{1,0:T(8,128)(2,1)} %get-tuple-element.58.o, ...), custom_call_target="tpu_custom_call" | custom-call | flops 26843545600 | bytes 67108864 | tf_op jit(solution)/shard_map/middle_layer_5/pallas_call | solution.py:1470
  146.9 108.8 %gate_up_grads_1.1 = (bf16[320,1600]{1,0:T(8,128)(2,1)}, bf16[320,1600]{1,0:T(8,128)(2,1)}, bf16[512,2560]{1,0:T(8,128)(2,1)}, bf16[512,640]{1,0:T(8,128)(2,1)}, f32[1,2560]{1,0:T(1,128)}) custom-call(bf16[512,2560]{1,0:T(8,128)(2,1)} %get-tuple-element.59.normed, bf16[512,1600]{1,0:T(8,128)(2,1)} %get-tuple-element.60.d_gate, ...), custom_call_target="tpu_custom_call" | custom-call | flops 10066329600 | bytes 29360128 | tf_op jit(solution)/shard_map/gate_up_grads_1/pallas_call | solution.py:880
  255.8 28.8 %attention_backward.1 = (bf16[512,960]{1,0:T(8,128)(2,1)}, bf16[4096,288]{1,0:T(8,128)(2,1)}, bf16[256,1280]{1,0:T(8,128)(2,1)}) custom-call(s32[2,8]{1,0:T(2,128)} %bitcast.43, s32[4]{0:T(128)} %lengths.5, bf16[2,10,256,256]{3,2,1,0:T(8,128)(2,1)} %get-tuple-element.53.qx, bf16[2,10,96,256]{3,2,1,0:T(8,128)(2,1)} %get-tuple-element.54.qt, ...), custom_call_target="tpu_custom_call" | custom-call | flops 21474836480 | bytes 25165824 | tf_op jit(solution)/shard_map/attention_backward/pallas_call | solution.py:403
  284.6 147.6 %up_tail_2.1 = (bf16[8,64,768]{2,1,0:T(8,128)(2,1)}, bf16[8,64,288]{2,1,0:T(8,128)(2,1)}, bf16[320,1600]{1,0:T(8,128)(2,1)}, bf16[320,640]{1,0:T(8,128)(2,1)}, b...) custom-call(bf16[4096,288]{1,0:T(8,128)(2,1)} %get-tuple-element.67.d_lat, ...), custom_call_target="tpu_custom_call" | custom-call | flops 7381975040 | bytes 33554432 | tf_op jit(solution)/shard_map/up_tail_2/pallas_call | solution.py:1071
  432.2 61.9 %down_tail_3.1 = (f32[512,2560]{1,0:T(8,128)}, bf16[320,768]{1,0:T(8,128)(2,1)}, bf16[320,288]{1,0:T(8,128)(2,1)}, bf16[32,128]{1,0:T(8,128)(2,1)}, bf16[8,16,2560]{2,1,0:T(8,128)(2,1)}) custom-call(bf16[512,768]{1,0:T(8,128)(2,1)} %bitcast.29, bf16[512,288]{1,0:T(8,128)(2,1)} %bitcast.31, f32[512,768]{1,0:T(8,128)} %get-tuple-element.78.q_pre, ...), custom_call_target="tpu_custom_call" | custom-call | flops 5536481280 | bytes 41943040 | tf_op jit(solution)/shard_map/down_tail_3/pallas_call | solution.py:1255
  494.0 0.0 copy-start.8
  494.0 0.0 copy-start.7
  494.0 0.0 copy-start.6
  494.1 0.0 copy-start.5
  494.1 0.0 copy-start.4
  494.1 3.5 pad_maximum_fusion
  497.6 0.0 copy-done.8
  497.6 0.6 slice.18
  498.2 0.5 slice.17
  498.7 0.7 fusion
  499.3 0.0 copy-done.7
  499.3 0.7 convert_element_type.28
  500.0 0.8 convert_element_type.27
  500.8 0.9 copy.31
  501.7 0.0 copy-done.4
  501.7 0.9 convert_element_type.29
  502.7 1.0 convert_element_type.25
  503.7 1.5 convert_element_type.32
  505.1 0.0 copy-done.1
  505.1 1.5 convert_element_type.30
  506.6 0.0 copy-done
  506.6 1.5 convert_element_type.31
  508.1 0.0 slice-done
  508.1 2.4 copy.33
  (13 shorter events, 0.0 us)
Async XLA Ops:
  494.0 3.5 copy-start.8
  494.0 5.3 %copy-start.7 = (bf16[32,1280]{1,0:T(8,128)(2,1)S(1)}, bf16[32,1280]{1,0:T(8,128)(2,1)}, u32[]{:S(2)}) copy-start(bf16[32,1280]{1,0:T(8,128)(2,1)} %get-tuple-element.86) | copy-start | bytes 245764
  494.0 6.0 %copy-start.6 = (bf16[96,960]{1,0:T(8,128)(2,1)S(1)}, bf16[96,960]{1,0:T(8,128)(2,1)}, u32[]{:S(2)}) copy-start(bf16[96,960]{1,0:T(8,128)(2,1)} %get-tuple-element.85) | copy-start | bytes 552964
  494.1 6.7 %copy-start.5 = (bf16[320,288]{1,0:T(8,128)(2,1)S(1)}, bf16[320,288]{1,0:T(8,128)(2,1)}, u32[]{:S(2)}) copy-start(bf16[320,288]{1,0:T(8,128)(2,1)} %get-tuple-element.84) | copy-start | bytes 552964
  494.1 7.6 %copy-start.4 = (bf16[320,640]{1,0:T(8,128)(2,1)S(1)}, bf16[320,640]{1,0:T(8,128)(2,1)}, u32[]{:S(2)}) copy-start(bf16[320,640]{1,0:T(8,128)(2,1)} %get-tuple-element.87) | copy-start | bytes 1228804
  497.6 5.1 copy-start.3
  497.6 6.1 %copy-start.2 = (bf16[320,1600]{1,0:T(8,128)(2,1)S(1)}, bf16[320,1600]{1,0:T(8,128)(2,1)}, u32[]{:S(2)}) copy-start(bf16[320,1600]{1,0:T(8,128)(2,1)} %get-tuple-element.90) | copy-start | bytes 3072004
  500.8 7.3 %slice-start = ((s8[5242880]{0:T(1024)(128)(4,1)}), s8[1048576]{0:T(1024)(128)(4,1)S(1)}, s32[]{:S(2)}) async-start(s8[5242880]{0:T(1024)(128)(4,1)} %bitcast.21), calls=%async_computation | async-start | bytes 2097152
  502.7 2.5 copy-start.1
  503.7 2.9 copy-start
  503.7 4.4 slice-start.1

commit v2 on v0

--- a/solution.py
+++ b/solution.py
@@ -912,66 +912,17 @@
     )(normed, d_gate, d_up, terms.reshape(chunked), tokens, attn, cot, gain_row, w_out)
 
 
-class FeedSum:
-    def __init__(self, tp, take, at, chunks, terms, tokens, attn, out):
-        own, landing, sums, self.tokens, self.attn, sems = take(6)
-        self.out = out
-        some = pl.ds(at, chunks)
-        pairs = ((terms, own), (tokens, self.tokens), (attn, self.attn))
-        self.loads = [
-            pltpu.make_async_copy(source.at[some], target, sems.at[k])
-            for k, (source, target) in enumerate(pairs)
-        ]
-        self.line = LineSum(tp, own, landing, sums, take(5), LAG)
-        self.ticks = self.line.ticks
-
-    def load(self):
-        for load in self.loads:
-            load.start()
-
-    def begin(self):
-        for load in self.loads:
-            load.wait()
-        self.line.leaves()
-
-    def duty(self, t):
-        self.line.duty(t)
-        c = self.line.landed(t)
-
-        @pl.when(self.line.inside(c))
-        def _():
-            both = self.attn[c].astype(jnp.float32) + self.line.total[c].astype(jnp.float32)
-            total = self.tokens[c].astype(jnp.float32) + RESIDUAL_SCALE * both
-            self.out[c] = total.astype(jnp.bfloat16)
-
-    def pump(self, first, last):
-        def body(t, carry):
-            self.duty(t)
-            return carry
-
-        lax.fori_loop(first, last, body, 0)
-
-
-def feed_scratch(chunks, width):
-    return [pltpu.VMEM((chunks, CHUNK, width), jnp.bfloat16)] * 5 + [
-        pltpu.SemaphoreType.DMA((3,)),
-        *line_sems(chunks),
-    ]
-
-
 TAIL_CHUNK = 64
 
 
 def up_tail_kernel(
-    n, tp, plans, feed_chunks, d_lat, d_query, w_qb, g_kvb, d_attn, ob, q_latent, d_feed, act,
-    f_part, tokens, attn, sum_q, sum_lat, down_out, out_out, qb_out, kvb_out, layer_out, *refs,
+    n, tp, plans, d_lat, d_query, w_qb, g_kvb, d_attn, ob, q_latent, d_feed, act,
+    sum_q, sum_lat, down_out, out_out, qb_out, kvb_out, *refs,
 ):
     take = taker(refs)
     own_q, land_q, own_lat, land_lat, d_attn_t, q_latent_t, d_feed_t = take(7)
     line_q = LineSum(tp, own_q, land_q, sum_q, take(5), LAG)
     line_lat = LineSum(tp, own_lat, land_lat, sum_lat, take(5), LAG)
-    feed = FeedSum(tp, take, 0, feed_chunks, f_part, tokens, attn, layer_out)
-    feed.load()
     chunk = own_q.shape[1]
 
     def store_lat(at, first, last, total):
@@ -1011,7 +962,6 @@
         lat.finish_step(step)
     line_lat.leaves()
     down.start_step(0)
-    feed.begin()
     chips = n // 2
     turn(d_attn, d_attn_t)
     out.start_core(line_q.duty)
@@ -1027,20 +977,15 @@
     steps = [(item, step) for step in range(lat.count - 1) for item in (down, out, kvb, qb)]
     q_share = spread(len(steps), line_q.ticks - 3 * chips)
     lat_share = spread(len(steps), line_lat.ticks - chips)
-    feed_share = spread(len(steps), feed.ticks)
-    for (item, step), (a, b), (c, d), (e, f) in zip(steps, q_share, lat_share, feed_share):
+    for (item, step), (a, b), (c, d) in zip(steps, q_share, lat_share):
         line_q.pump(3 * chips + a, 3 * chips + b)
         line_lat.pump(chips + c, chips + d)
-        feed.pump(e, f)
         item.finish_step(step)
-    for item in (*plans, line_q, line_lat, feed.line):
+    for item in (*plans, line_q, line_lat):
         item.drain()
 
 
-def up_tail(
-    n, tp, d_lat, d_query, w_qb, g_kvb, d_attn, ob, q_latent, d_feed, act, f_part, tokens, attn,
-    feed_chunks, collective_id,
-):
+def up_tail(n, tp, d_lat, d_query, w_qb, g_kvb, d_attn, ob, q_latent, d_feed, act, collective_id):
     rows, width = d_attn.shape
     rank = q_latent.shape[1]
     hidden = act.shape[1]
@@ -1056,18 +1001,15 @@
     ]
     q_shape = (rows // TAIL_CHUNK, TAIL_CHUNK, rank)
     lat_shape = (rows // TAIL_CHUNK, TAIL_CHUNK, lat_width)
-    anywhere = pl.BlockSpec(memory_space=pl.ANY)
-    chunked = (-1, CHUNK, width)
-    sum_q, sum_lat, *grads, layer_out = pl.pallas_call(
-        functools.partial(up_tail_kernel, n, tp, plans, feed_chunks),
+    sum_q, sum_lat, *grads = pl.pallas_call(
+        functools.partial(up_tail_kernel, n, tp, plans),
         out_shape=(
             jax.ShapeDtypeStruct(q_shape, half),
             jax.ShapeDtypeStruct(lat_shape, half),
             *[jax.ShapeDtypeStruct((plan.rows, plan.columns), half) for plan in plans[1:]],
-            jax.ShapeDtypeStruct((feed_chunks, CHUNK, width), half),
-        ),
-        in_specs=[vmem] * 9 + [anywhere] * 3,
-        out_specs=(vmem,) * 7,
+        ),
+        in_specs=[vmem] * 9,
+        out_specs=(vmem,) * 6,
         scratch_shapes=[
             pltpu.VMEM(q_shape, half),
             pltpu.VMEM(q_shape, half),
@@ -1078,7 +1020,6 @@
             pltpu.VMEM((width, rows), half),
             *line_sems(rows // TAIL_CHUNK),
             *line_sems(rows // TAIL_CHUNK),
-            *feed_scratch(feed_chunks, width),
             *[shape for plan in plans for shape in plan.scratch()],
         ],
         compiler_params=pltpu.CompilerParams(
@@ -1090,46 +1031,26 @@
             transcendentals=0,
         ),
         name=f"up_tail_{collective_id}",
-    )(
-        d_lat,
-        d_query,
-        w_qb,
-        g_kvb,
-        d_attn,
-        ob,
-        q_latent,
-        d_feed,
-        act,
-        *[array.reshape(chunked) for array in (f_part, tokens, attn)],
-    )
-    return (
-        sum_q.reshape(rows, rank),
-        sum_lat.reshape(rows, lat_width),
-        *grads,
-        layer_out.reshape(-1, width),
-    )
+    )(d_lat, d_query, w_qb, g_kvb, d_attn, ob, q_latent, d_feed, act)
+    return sum_q.reshape(rows, rank), sum_lat.reshape(rows, lat_width), *grads
 
 
 def down_tail_kernel(
-    n, tp, plans, feed_chunks, sum_q, sum_lat, q_pre, lat_raw, tokens, d_attn, gain_row, g_mid, w_qa,
-    w_kva, cos, sin, f_part, tokens_chunked, attn, grad_in, qa_out, kva_out, gains_out, layer_out,
-    d_q, d_kv, normed_t, scales, g_in, g_q, g_kv, packed, packing, grad_slots, out_sems, *refs,
+    n, plans, sum_q, sum_lat, q_pre, lat_raw, tokens, d_attn, gain_row, g_mid, w_qa, w_kva, cos, sin, grad_in, qa_out, kva_out, gains_out,
+    d_q, d_kv, normed_t, scales, g_in, g_q, g_kv, packed, packing, grad_slots, out_sems,
+    *refs,
 ):
     take = taker(refs)
     qa, kva, gains = plans
     qa.bind(take, (normed_t, d_q), store_in(qa_out))
     kva.bind(take, (normed_t, d_kv), store_in(kva_out))
     gains.bind(take, packed, store_in(gains_out))
-    at = f_part.shape[0] - feed_chunks
-    feed = FeedSum(tp, take, at, feed_chunks, f_part, tokens_chunked, attn, layer_out)
-    feed.load()
     rows = tokens.shape[0]
     block = rows // 4
     gain_in, _, gain_q, gain_kv = split_gains(gain_row, tokens.shape[1], q_pre.shape[1])
     lane = lax.broadcasted_iota(jnp.int32, (block, HEAD), 1)
     barrier = pltpu.get_barrier_semaphore()
     others = greet_ctx(n, barrier)
-    feed.line.greet(barrier)
 
     def rows_of(k):
         return pl.ds(pl.multiple_of(k * block, block), block)
@@ -1139,8 +1060,6 @@
             grad_slots.at[slot], grad_in.at[rows_of(k), :], out_sems.at[slot]
         )
 
-    feed.line.wait_greetings(barrier, others)
-    feed.begin()
     for ref in (g_in, g_q, g_kv):
         ref[...] = jnp.zeros(ref.shape, jnp.float32)
 
@@ -1171,17 +1090,15 @@
         return carry
 
     lax.fori_loop(0, 4, norms, 0)
-    chips = n // 2
+    pl.semaphore_wait(barrier, others)
     qa.start_core()
     kva.start_core()
     qa.finish_core()
     qa.start_step(0)
-    kva.finish_core(feed.duty)
+    kva.finish_core()
     kva.start_step(0)
-    shares = [(chips + a, chips + b) for a, b in spread(4 + 3, feed.ticks - chips)]
     for k in range(4):
         at = pl.ds(k * block, block)
-        feed.pump(*shares[k])
         if k >= 2:
             deliver(k - 2, k % 2).wait()
         d_normed = dot_nt(d_q[at, :], w_qa[...]) + dot_nn(d_kv[at, :], w_kva[...])
@@ -1207,23 +1124,20 @@
         at += share
     packed[...] = packing[...].astype(jnp.bfloat16)
     gains.start_core()
-    feed.pump(*shares[4])
     gains.finish_core()
     gains.start_step(0)
-    feed.pump(*shares[5])
-    feed.pump(*shares[6])
     for step in range(qa.count - 1):
         for item in (qa, kva, gains):
             item.finish_step(step)
     deliver(2, 0).wait()
     deliver(3, 1).wait()
-    for item in (*plans, feed.line):
+    for item in plans:
         item.drain()
 
 
 def down_tail(
-    n, tp, sum_q, sum_lat, q_pre, lat_raw, tokens, d_attn, gain_row, g_mid, w_qa, w_kva, cos, sin,
-    f_part, attn, feed_chunks, collective_id,
+    n, sum_q, sum_lat, q_pre, lat_raw, tokens, d_attn, gain_row, g_mid, w_qa, w_kva, cos, sin,
+    collective_id,
 ):
     rows, width = tokens.shape
     rank = q_pre.shape[1]
@@ -1239,16 +1153,14 @@
         Scatter(n, lines, HEAD, True),
     ]
     slots = pltpu.VMEM((2, rows // 4, width), full)
-    chunked = (-1, CHUNK, width)
-    grad_in, qa, kva, gains, layer_out = pl.pallas_call(
-        functools.partial(down_tail_kernel, n, tp, plans, feed_chunks),
+    grad_in, qa, kva, gains = pl.pallas_call(
+        functools.partial(down_tail_kernel, n, plans),
         out_shape=(
             jax.ShapeDtypeStruct((rows, width), full),
             *[jax.ShapeDtypeStruct((plan.rows, plan.columns), half) for plan in plans],
-            jax.ShapeDtypeStruct((feed_chunks, CHUNK, width), half),
-        ),
-        in_specs=[vmem] * 12 + [anywhere] * 3,
-        out_specs=(anywhere, vmem, vmem, vmem, vmem),
+        ),
+        in_specs=[vmem] * 12,
+        out_specs=(anywhere, vmem, vmem, vmem),
         scratch_shapes=[
             pltpu.VMEM((rows, rank), half),
             pltpu.VMEM((rows, KVR + ROPE), half),
@@ -1262,7 +1174,6 @@
             slots,
             dma((2,)),
             *[shape for plan in plans for shape in plan.scratch()],
-            *feed_scratch(feed_chunks, width),
         ],
         compiler_params=pltpu.CompilerParams(
             vmem_limit_bytes=MIDDLE_VMEM, collective_id=collective_id, has_side_effects=True
@@ -1286,14 +1197,12 @@
         w_kva,
         cos,
         sin,
-        *[array.reshape(chunked) for array in (f_part, tokens, attn)],
     )
     gains = gains.astype(full).reshape(-1)
     ends = [0]
     for size in (width, width, rank, KVR):
         ends.append(ends[-1] + size // n)
-    own_gains = [gains[first:last] for first, last in zip(ends, ends[1:])]
-    return grad_in, qa, kva, own_gains, layer_out.reshape(-1, width)
+    return grad_in, qa, kva, [gains[first:last] for first, last in zip(ends, ends[1:])]
 
 
 CHUNK = 16
@@ -1751,21 +1660,28 @@
         devices, lax.axis_size("tp"), normed_mid, d_gate, d_up, d_part, tokens_in, attention,
         cotangent, gains, w_out, 1,
     )
+    d_heads, feed_part = lax.optimization_barrier((d_heads, feed_part))
+    feed_own = lax.psum_scatter(feed_part, "tp", scatter_dimension=0, tiled=True)
+    own_rows = feed_own.shape[0]
+    own_at = lax.axis_index("tp") * own_rows
+    tokens_own = lax.dynamic_slice_in_dim(tokens_in, own_at, own_rows, 0).astype(jnp.float32)
+    attention_own = lax.dynamic_slice_in_dim(attention, own_at, own_rows, 0).astype(jnp.float32)
+    middle_own = tokens_own + RESIDUAL_SCALE * attention_own
+    out_own = (middle_own + RESIDUAL_SCALE * feed_own.astype(jnp.float32)).astype(jnp.bfloat16)
     d_query_pre, d_latents, gw_kvb = attention_backward(
         block_map, doc_lengths, queries, queries_t, log_totals, attn_f, d_heads, latents, w_kvb,
         cosine, sine,
     )
-    chunks = tokens_in.shape[0] // CHUNK
-    sum_q, sum_lat, gw_down, gw_out, gw_qb, gw_kvb, out_first = up_tail(
+    sum_q, sum_lat, gw_down, gw_out, gw_qb, gw_kvb = up_tail(
         devices, lax.axis_size("tp"), d_latents, d_query_pre, w_qb.T, gw_kvb, d_attention, heads_out,
-        q_latent, d_feed, activation, feed_part, tokens_in, attention, chunks // 2, 2,
+        q_latent, d_feed, activation, 2,
     )
-    grad_in, gw_qa, gw_kva, own_gains, out_second = down_tail(
-        devices, lax.axis_size("tp"), sum_q, sum_lat, q_latent_pre, latent_raw, tokens_in,
-        d_attention, gains, d_gain_mid, w_qa, w_kva.T, cosine, sine, feed_part, attention,
-        chunks - chunks // 2, 3,
+    sum_q, out_own = lax.optimization_barrier((sum_q, out_own))
+    out = lax.all_gather(out_own, "tp", axis=0, tiled=True)
+    grad_in, gw_qa, gw_kva, own_gains = down_tail(
+        devices, sum_q, sum_lat, q_latent_pre, latent_raw, tokens_in, d_attention, gains,
+        d_gain_mid, w_qa, w_kva.T, cosine, sine, 3,
     )
-    out = jnp.concatenate([out_first, out_second], axis=0)
     grads = (gw_qa, gw_kva, gw_qb, gw_kvb, gw_out, gw_gate, gw_up, gw_down)
     return (
         out,

time: 505 us -> 484 us (0.958)
  Pallas kernels: 479 us -> 438 us
  between operations: 1.19 us -> 14.5 us
    pallas_call x2, Pallas kernels: 174 us -> 137 us  [the longest x1 94.9 us: up_tail(): pl.pallas_call(functools.partial(up_tail_kernel, n, tp, plans), out_shape...]
    pallas_call x1, Pallas kernels: 55 us -> 49.8 us  [attention_backward(): pl.pallas_call(functools.partial(backward_kernel, blocks, heads), out_sha...]
  transfers between devices with their start and end apart: 0 -> 2, of which waited for: 0 -> 1; matrix products, arithmetic and copies ran while one was open for 0% -> 3% of each run, Pallas kernels for 0% -> 39%
where the time goes in v2:
time: 484 us; the launch traced here: 476 us
  Pallas kernels  438 us (90%)
  between operations  14.5 us (3%)
  other arithmetic  13.7 us (3%)
  local copies, waits for them, and re-layouts  9.91 us (2%)
    pallas_call x1, Pallas kernels, middle_layer(): pl.pallas_call(functools.partial(middle_kernel, n, LAG), out_shape=(jax.S...  97.4 us
    pallas_call x1, Pallas kernels, up_tail(): pl.pallas_call(functools.partial(up_tail_kernel, n, tp, plans), out_shape...  94.9 us
    pallas_call x1, Pallas kernels, gate_up_grads(): pl.pallas_call(functools.partial(gate_up_kernel, n, tp, plans), out_shape...  93 us
    pallas_call x1, Pallas kernels, attention_backward(): pl.pallas_call(functools.partial(backward_kernel, blocks, heads), out_sha...  49.8 us
    pallas_call x1, Pallas kernels, down_tail(): pl.pallas_call(functools.partial(down_tail_kernel, n, plans), out_shape=(...  42.2 us
    pallas_call x1, Pallas kernels, head_layer(): pl.pallas_call(functools.partial(head_kernel, n), out_shape=(jax.ShapeDty...  33.5 us
    pallas_call x1, Pallas kernels, attention_forward(): pl.pallas_call(functools.partial(forward_kernel, blocks, heads), out_shap...  26.7 us
  transfers between devices with their start and end apart: 2, of which 1 were waited for; matrix products, arithmetic and copies ran while one was open for 3% of the time, Pallas kernels for 39%

profile of v2, /device:TPU:0, one launch (start us, length us, event | category | flops | bytes accessed | tf_op | source)
XLA Modules:
  0.0 476.4 jit_solution(15508484537921462978)
XLA Ops:
  7.2 0.0 reduce-scatter.2.cloned.1.call-start
  7.2 1.4 pad_maximum_fusion
  8.6 33.5 %head_layer_0.1 = (bf16[8,512,288]{2,1,0:T(8,128)(2,1)}, bf16[512,768]{1,0:T(8,128)(2,1)}, f32[512,768]{1,0:T(8,128)}, f32[512,256]{1,0:T(8,128)}, f32[512,128]{...) custom-call(s32[2,8]{1,0:T(2,128)} %bitcast.28, s32[4]{0:T(128)} %lengths.5, ...), custom_call_target="tpu_custom_call" | custom-call | flops 2768240640 | bytes 25165824 | tf_op jit(solution)/shard_map/head_layer_0/pallas_call | solution.py:1581
  42.1 26.7 %attention_forward.1 = (f32[512,640]{1,0:T(8,128)}, bf16[512,640]{1,0:T(8,128)(2,1)}, f32[2,16,256]{2,1,0:T(8,128)}) custom-call(s32[2,8]{1,0:T(2,128)} %bitcast.29, s32[4]{0:T(128)} %lengths.5, bf16[2,10,256,256]{3,2,1,0:T(8,128)(2,1)} %get-tuple-element.55.qx, bf16[4096,288]{1,0:T(8,128)(2,1)} %bitcast.31, bf16[256,1280]{1,0:T(8,128)(2,1)} %wkvb.3), custom_call_target="tpu_custom_call" | custom-call | flops 10737418240 | bytes 16777216 | tf_op jit(solution)/shard_map/attention_forward/pallas_call | solution.py:208
  68.8 97.4 %middle_layer_5.1 = (bf16[32,16,2560]{2,1,0:T(8,128)(2,1)}, bf16[512,2560]{1,0:T(8,128)(2,1)}, bf16[512,2560]{1,0:T(8,128)(2,1)}, bf16[512,1600]{1,0:T(8,128)(2,...) custom-call(bf16[512,640]{1,0:T(8,128)(2,1)} %get-tuple-element.60.o, ...), custom_call_target="tpu_custom_call" | custom-call | flops 26843545600 | bytes 67108864 | tf_op jit(solution)/shard_map/middle_layer_5/pallas_call | solution.py:1367
  166.2 93.0 %gate_up_grads_1.1 = (bf16[320,1600]{1,0:T(8,128)(2,1)}, bf16[320,1600]{1,0:T(8,128)(2,1)}, bf16[512,2560]{1,0:T(8,128)(2,1)}, bf16[512,640]{1,0:T(8,128)(2,1)}, f32[1,2560]{1,0:T(1,128)}) custom-call(bf16[512,2560]{1,0:T(8,128)(2,1)} %get-tuple-element.61.normed, bf16[512,1600]{1,0:T(8,128)(2,1)} %get-tuple-element.62.d_gate, ...), custom_call_target="tpu_custom_call" | custom-call | flops 10066329600 | bytes 29360128 | tf_op jit(solution)/shard_map/gate_up_grads_1/pallas_call | solution.py:880
  259.3 0.0 reduce-scatter.2.cloned.1.call-update
  259.3 0.2 all-gather.2.cloned.1.call-start
  259.5 49.8 %attention_backward.1 = (bf16[512,960]{1,0:T(8,128)(2,1)}, bf16[4096,288]{1,0:T(8,128)(2,1)}, bf16[256,1280]{1,0:T(8,128)(2,1)}) custom-call(s32[2,8]{1,0:T(2,128)} %bitcast.30, s32[4]{0:T(128)} %lengths.5, bf16[2,10,256,256]{3,2,1,0:T(8,128)(2,1)} %get-tuple-element.55.qx, bf16[2,10,96,256]{3,2,1,0:T(8,128)(2,1)} %get-tuple-element.56.qt, ...), custom_call_target="tpu_custom_call" | custom-call | flops 21474836480 | bytes 25165824 | tf_op jit(solution)/shard_map/attention_backward/pallas_call | solution.py:403
  309.3 94.9 %up_tail_2.1 = (bf16[8,64,768]{2,1,0:T(8,128)(2,1)}, bf16[8,64,288]{2,1,0:T(8,128)(2,1)}, bf16[320,1600]{1,0:T(8,128)(2,1)}, bf16[320,640]{1,0:T(8,128)(2,1)}, b...) custom-call(bf16[4096,288]{1,0:T(8,128)(2,1)} %get-tuple-element.71.d_lat, bf16[512,960]{1,0:T(8,128)(2,1)} %get-tuple-element.72.d_query, ...), custom_call_target="tpu_custom_call" | custom-call | flops 7381975040 | bytes 33554432 | tf_op jit(solution)/shard_map/up_tail_2/pallas_call | solution.py:1004
  404.2 0.0 copy-start.5
  404.3 0.0 copy-start.6
  404.3 0.0 reduce-scatter.2.cloned.1.call-done
  404.3 2.8 add_convert_fusion
  407.1 0.0 all-gather.2.cloned.1.call-update
  407.1 0.8 convert_element_type.43
  407.9 0.7 convert_element_type.44
  408.6 0.9 convert_element_type.45
  409.5 1.5 convert_element_type.46
  411.0 1.5 convert_element_type.47
  412.5 1.5 convert_element_type.48
  414.0 42.2 %down_tail_3.1 = (f32[512,2560]{1,0:T(8,128)}, bf16[320,768]{1,0:T(8,128)(2,1)}, bf16[320,288]{1,0:T(8,128)(2,1)}, bf16[32,128]{1,0:T(8,128)(2,1)}) custom-call(bf16[512,768]{1,0:T(8,128)(2,1)} %bitcast.34, bf16[512,288]{1,0:T(8,128)(2,1)} %bitcast.35, f32[512,768]{1,0:T(8,128)} %get-tuple-element.83.q_pre, f32[512,256]{1,0:T(8,128)} %get-tuple-element.84.lat_raw, ...), custom_call_target="tpu_custom_call" | custom-call | flops 5536481280 | bytes 41943040 | tf_op jit(solution)/shard_map/down_tail_3/pallas_call | solution.py:1156
  456.2 0.7 bitcast_convert_fusion
  456.9 0.5 slice.17
  457.4 0.6 slice.18
  458.0 2.0 convert_element_type.41
  460.0 1.9 copy.31
  461.8 0.7 fusion
  462.5 0.4 all-gather.2.cloned.1.call-done
  462.9 3.6 copy.34
  466.4 0.4 copy-done
  466.8 2.4 copy.35
  (11 shorter events, 0.0 us)
Async XLA Ops:
  7.2 397.1 %reduce-scatter.2.cloned.1.call-start = ((), (), s32[]{:S(2)}) async-start(), calls=%async_computation.1 | async-start | bytes 3276800 | tf_op jit(solution)/shard_map/reduce_scatter | solution.py:1664
  259.3 203.6 %all-gather.2.cloned.1.call-start = ((), (), s32[]{:S(2)}) async-start(), calls=%async_computation.2 | async-start | bytes 3276800 | tf_op jit(solution)/shard_map/all_gather | solution.py:1680
  404.2 2.9 copy-start.5
  404.3 3.7 copy-start.6
  404.3 4.3 copy-start.4
  404.3 5.3 %copy-start.2 = (bf16[320,1600]{1,0:T(8,128)(2,1)S(1)}, bf16[320,1600]{1,0:T(8,128)(2,1)}, u32[]{:S(2)}) copy-start(bf16[320,1600]{1,0:T(8,128)(2,1)} %get-tuple-element.92) | copy-start | bytes 3072004
  407.1 3.9 copy-start.1
  409.5 2.9 copy-start.3
  462.8 3.9 copy-start
Sparse Core Ops, SparseCore 0:
  259.4 54.3 reduce-scatter.1
  407.2 55.5 all-gather.1

commit v3 on v2

--- a/solution.py
+++ b/solution.py
@@ -789,11 +789,12 @@
 
 
 def gate_up_kernel(
-    n, tp, plans, normed, d_gate, d_up, terms, tokens, attn, cot, gain_row, w_out,
+    n, tp, plans, normed, d_gate, d_up, terms, tokens, attn, cot, w_out_in, gain_row,
     gate_out, up_out, d_attn, d_heads, g_mid, *refs,
 ):
     take = taker(refs)
-    own, landing, sums, normed_t, slots, in_sems, own_sem = take(7)
+    own, landing, sums, normed_t, slots, in_sems, own_sem, w_out, w_sem = take(9)
+    w_load = pltpu.make_async_copy(w_out_in, w_out, w_sem)
     line = LineSum(tp, own, landing, sums, take(5), LAG)
     gate = plans[0].bind(take, (normed_t, d_gate), store_in(gate_out))
     up = plans[1].bind(take, (normed_t, d_up), store_in(up_out))
@@ -818,9 +819,12 @@
     for b in range(min(2, blocks)):
         for copy in fetch(b):
             copy.start()
+    w_load.start()
     g_mid[...] = jnp.zeros(g_mid.shape, jnp.float32)
 
     def norm(b):
+        if b == 0:
+            w_load.wait()
         for copy in fetch(b):
             copy.wait()
         for part in range(0, BLOCK, 2 * CHUNK):
@@ -886,7 +890,7 @@
             jax.ShapeDtypeStruct((rows, head_width), half),
             jax.ShapeDtypeStruct((1, width), jnp.float32),
         ),
-        in_specs=[vmem] * 3 + [anywhere] * 4 + [vmem] * 2,
+        in_specs=[vmem] * 3 + [anywhere] * 5 + [vmem],
         out_specs=(vmem,) * 5,
         scratch_shapes=[
             pltpu.VMEM(chunked, half),
@@ -896,6 +900,8 @@
             pltpu.VMEM((2, 3, BLOCK, width), half),
             pltpu.SemaphoreType.DMA((2, 3)),
             pltpu.SemaphoreType.DMA,
+            pltpu.VMEM(w_out.shape, half),
+            pltpu.SemaphoreType.DMA,
             *line_sems(rows // CHUNK),
             *plans[0].scratch(),
             *plans[1].scratch(),
@@ -909,18 +915,25 @@
             transcendentals=0,
         ),
         name=f"gate_up_grads_{collective_id}",
-    )(normed, d_gate, d_up, terms.reshape(chunked), tokens, attn, cot, gain_row, w_out)
+    )(normed, d_gate, d_up, terms.reshape(chunked), tokens, attn, cot, w_out, gain_row)
 
 
 TAIL_CHUNK = 64
 
 
 def up_tail_kernel(
-    n, tp, plans, d_lat, d_query, w_qb, g_kvb, d_attn, ob, q_latent, d_feed, act,
+    n, tp, plans, d_lat, d_query, w_qb, g_kvb_in, d_attn_in, ob_in, q_latent_in, d_feed_in, act_in,
     sum_q, sum_lat, down_out, out_out, qb_out, kvb_out, *refs,
 ):
     take = taker(refs)
     own_q, land_q, own_lat, land_lat, d_attn_t, q_latent_t, d_feed_t = take(7)
+    g_kvb, d_attn, ob, q_latent, d_feed, act, in_sems = take(7)
+    loads = {}
+    pairs = ((d_feed_in, d_feed), (act_in, act), (d_attn_in, d_attn), (ob_in, ob))
+    pairs += ((q_latent_in, q_latent), (g_kvb_in, g_kvb))
+    for k, (source, target) in enumerate(pairs):
+        loads[id(target)] = pltpu.make_async_copy(source, target, in_sems.at[k])
+        loads[id(target)].start()
     line_q = LineSum(tp, own_q, land_q, sum_q, take(5), LAG)
     line_lat = LineSum(tp, own_lat, land_lat, sum_lat, take(5), LAG)
     chunk = own_q.shape[1]
@@ -954,7 +967,9 @@
     lax.fori_loop(0, own_q.shape[0] // 2, query, 0)
     lat.finish_core()
     lat.start_step(0)
+    loads[id(d_feed)].wait()
     turn(d_feed, d_feed_t)
+    loads[id(act)].wait()
     down.start_core()
     lat.finish_step(0)
     down.finish_core()
@@ -963,11 +978,15 @@
     line_lat.leaves()
     down.start_step(0)
     chips = n // 2
+    loads[id(d_attn)].wait()
     turn(d_attn, d_attn_t)
+    loads[id(ob)].wait()
     out.start_core(line_q.duty)
     out.finish_core(lambda chip: line_q.duty(chips + chip))
     out.start_step(0)
+    loads[id(g_kvb)].wait()
     kvb.start_core()
+    loads[id(q_latent)].wait()
     turn(q_latent, q_latent_t)
     qb.start_core(lambda chip: line_q.duty(2 * chips + chip))
     kvb.finish_core()
@@ -1008,7 +1027,7 @@
             jax.ShapeDtypeStruct(lat_shape, half),
             *[jax.ShapeDtypeStruct((plan.rows, plan.columns), half) for plan in plans[1:]],
         ),
-        in_specs=[vmem] * 9,
+        in_specs=[vmem] * 3 + [pl.BlockSpec(memory_space=pl.ANY)] * 6,
         out_specs=(vmem,) * 6,
         scratch_shapes=[
             pltpu.VMEM(q_shape, half),
@@ -1018,6 +1037,8 @@
             pltpu.VMEM((width, rows), half),
             pltpu.VMEM((rank, rows), half),
             pltpu.VMEM((width, rows), half),
+            *[pltpu.VMEM(late.shape, half) for late in (g_kvb, d_attn, ob, q_latent, d_feed, act)],
+            pltpu.SemaphoreType.DMA((6,)),
             *line_sems(rows // TAIL_CHUNK),
             *line_sems(rows // TAIL_CHUNK),
             *[shape for plan in plans for shape in plan.scratch()],
@@ -1036,12 +1057,19 @@
 
 
 def down_tail_kernel(
-    n, plans, sum_q, sum_lat, q_pre, lat_raw, tokens, d_attn, gain_row, g_mid, w_qa, w_kva, cos, sin, grad_in, qa_out, kva_out, gains_out,
-    d_q, d_kv, normed_t, scales, g_in, g_q, g_kv, packed, packing, grad_slots, out_sems,
+    n, plans, sum_q, sum_lat, q_pre, lat_raw, tokens, d_attn_in, gain_row, g_mid, w_qa_in, w_kva_in, cos, sin, grad_in, qa_out, kva_out, gains_out,
+    d_q, d_kv, normed_t, scales, g_in, g_q, g_kv, packed, packing, grad_slots, out_sems, d_attn, w_qa, w_kva, in_sems,
     *refs,
 ):
     take = taker(refs)
     qa, kva, gains = plans
+    pairs = ((w_qa_in, w_qa), (w_kva_in, w_kva), (d_attn_in, d_attn))
+    loads = [
+        pltpu.make_async_copy(source, target, in_sems.at[k])
+        for k, (source, target) in enumerate(pairs)
+    ]
+    for load in loads:
+        load.start()
     qa.bind(take, (normed_t, d_q), store_in(qa_out))
     kva.bind(take, (normed_t, d_kv), store_in(kva_out))
     gains.bind(take, packed, store_in(gains_out))
@@ -1097,6 +1125,8 @@
     qa.start_step(0)
     kva.finish_core()
     kva.start_step(0)
+    for load in loads:
+        load.wait()
     for k in range(4):
         at = pl.ds(k * block, block)
         if k >= 2:
@@ -1159,7 +1189,11 @@
             jax.ShapeDtypeStruct((rows, width), full),
             *[jax.ShapeDtypeStruct((plan.rows, plan.columns), half) for plan in plans],
         ),
-        in_specs=[vmem] * 12,
+        in_specs=[vmem] * 5
+        + [anywhere]
+        + [vmem] * 2
+        + [anywhere] * 2
+        + [vmem] * 2,
         out_specs=(anywhere, vmem, vmem, vmem),
         scratch_shapes=[
             pltpu.VMEM((rows, rank), half),
@@ -1173,6 +1207,10 @@
             pltpu.VMEM((n * lines, HEAD), full),
             slots,
             dma((2,)),
+            pltpu.VMEM((rows, width), half),
+            pltpu.VMEM(w_qa.shape, half),
+            pltpu.VMEM(w_kva.shape, half),
+            dma((3,)),
             *[shape for plan in plans for shape in plan.scratch()],
         ],
         compiler_params=pltpu.CompilerParams(
@@ -1446,12 +1484,27 @@
 
 
 def head_kernel(
-    n, block_map, lengths, tokens, gains, rates, w_qa, w_kva, w_qb,
-    out, q_latent, q_pre, lat_raw, cos, sin, qx, qt,
+    n, block_map, lengths, tokens, gains, rates, w_qa_in, w_kva, w_qb_in,
+    out, q_latent_to, q_pre_to, lat_raw_to, cos_to, sin_to, qx_to, qt_to,
+    q_latent, q_pre, lat_raw, cos, sin, qx, qt, w_qa, w_qb, in_sems, out_sems,
     own, normed, w_rope, flat, local_sem, step_sends, step_lands, core_sends, core_lands,
 ):
     gain_in, _, gain_q, gain_kv = split_gains(gains, tokens.shape[1], w_qa.shape[1])
     heads = qx.shape[1]
+    loads = [
+        pltpu.make_async_copy(w_qa_in, w_qa, in_sems.at[0]),
+        pltpu.make_async_copy(w_qb_in, w_qb, in_sems.at[1]),
+    ]
+    for load in loads:
+        load.start()
+    kept = []
+
+    def keep(*pairs):
+        for source, target in pairs:
+            copy = pltpu.make_async_copy(source, target, out_sems.at[len(kept)])
+            copy.start()
+            kept.append(copy)
+
     count = n.bit_length() - 1
     me = lax.axis_index("ctx")
     rows = own.shape[0]
@@ -1486,6 +1539,7 @@
         own[at, KVR:] = rope[:, :ROPE].astype(jnp.bfloat16)
         return carry
 
+    keep((cos, cos_to), (sin, sin_to))
     lax.fori_loop(0, 4, latents, 0)
     pl.semaphore_wait(barrier, count)
     local = pltpu.make_async_copy(own, out.at[me], local_sem)
@@ -1535,6 +1589,7 @@
             qx[j, h, :, HEAD:] = rope.astype(jnp.bfloat16)
             qt[j, h, :NOPE, :] = nope.T[:NOPE, :].astype(jnp.bfloat16)
             qt[j, h, NOPE:, :] = rope.T[:ROPE, :].astype(jnp.bfloat16)
+        keep((qx.at[j], qx_to.at[j]), (qt.at[j], qt_to.at[j]))
 
     started = []
     for step in range(count - 1):
@@ -1548,8 +1603,12 @@
                 started.append(copy)
         if step == 0:
             core_copy(me, 0, True).start()
+            keep((lat_raw, lat_raw_to))
+            for load in loads:
+                load.wait()
         lax.fori_loop(min(2 * step, 4), min(2 * step + 2, 4) if step < count - 2 else 4, query, 0)
         if step == count - 2:
+            keep((q_pre, q_pre_to), (q_latent, q_latent_to))
             queries(0)
         for part, order in enumerate(orders):
             for slot in range(1 << step):
@@ -1564,6 +1623,8 @@
     for chip in range(n // 2):
         core_copy(me, chip, chip == 0).wait_send()
     local.wait()
+    for copy in kept:
+        copy.wait()
 
 
 def head_layer(n, block_map, lengths, tokens, gains, w_qa, w_kva, w_qb, collective_id):
@@ -1574,6 +1635,7 @@
     slots = max(n // 4, 1)
     dma = pltpu.SemaphoreType.DMA
     smem = pl.BlockSpec(memory_space=pltpu.SMEM)
+    anywhere = pl.BlockSpec(memory_space=pl.ANY)
     heads = w_qb.shape[0] // (NOPE + ROPE)
     pairs = (2, heads)
     lane = np.arange(HEAD)
@@ -1590,9 +1652,20 @@
             jax.ShapeDtypeStruct((*pairs, rows // 2, WIDE), jnp.bfloat16),
             jax.ShapeDtypeStruct((*pairs, NOPE + ROPE, rows // 2), jnp.bfloat16),
         ),
-        in_specs=[smem] * 2 + [vmem] * 6,
-        out_specs=(vmem,) * 8,
+        in_specs=[smem] * 2 + [vmem] * 3 + [anywhere, vmem, anywhere],
+        out_specs=(vmem,) + (anywhere,) * 7,
         scratch_shapes=[
+            pltpu.VMEM((rows, rank), jnp.bfloat16),
+            pltpu.VMEM((rows, rank), jnp.float32),
+            pltpu.VMEM((rows, KVR), jnp.float32),
+            pltpu.VMEM((rows, HEAD), jnp.float32),
+            pltpu.VMEM((rows, HEAD), jnp.float32),
+            pltpu.VMEM((*pairs, rows // 2, WIDE), jnp.bfloat16),
+            pltpu.VMEM((*pairs, NOPE + ROPE, rows // 2), jnp.bfloat16),
+            pltpu.VMEM(w_qa.shape, jnp.bfloat16),
+            pltpu.VMEM(w_qb.shape, jnp.bfloat16),
+            dma((2,)),
+            dma((9,)),
             pltpu.VMEM((rows, KVR + ROPE), jnp.bfloat16),
             pltpu.VMEM((rows, width), jnp.bfloat16),
             pltpu.VMEM((HEAD, width), jnp.bfloat16),

time: 484 us -> 470 us (0.971)
  Pallas kernels: 438 us -> 422 us
    pallas_call x1, Pallas kernels: 49.8 us -> 38.9 us  [attention_backward(): pl.pallas_call(functools.partial(backward_kernel, blocks, heads), out_sha...]
    pallas_call x1, Pallas kernels: 26.7 us -> 20.3 us  [attention_forward(): pl.pallas_call(functools.partial(forward_kernel, blocks, heads), out_shap...]
  transfers between devices with their start and end apart: 2 -> 2, of which waited for: 1 -> 1; matrix products, arithmetic and copies ran while one was open for 3% -> 3% of each run, Pallas kernels for 39% -> 38%
where the time goes in v3:
time: 470 us; the launch traced here: 463 us
  Pallas kernels  422 us (90%)
  between operations  14.5 us (3%)
  other arithmetic  13.7 us (3%)
  local copies, waits for them, and re-layouts  9.91 us (2%)
    pallas_call x1, Pallas kernels, up_tail(): pl.pallas_call(functools.partial(up_tail_kernel, n, tp, plans), out_shape...  99 us
    pallas_call x1, Pallas kernels, middle_layer(): pl.pallas_call(functools.partial(middle_kernel, n, LAG), out_shape=(jax.S...  97.4 us
    pallas_call x1, Pallas kernels, gate_up_grads(): pl.pallas_call(functools.partial(gate_up_kernel, n, tp, plans), out_shape...  96.2 us
    pallas_call x1, Pallas kernels, down_tail(): pl.pallas_call(functools.partial(down_tail_kernel, n, plans), out_shape=(...  39.3 us
    pallas_call x1, Pallas kernels, attention_backward(): pl.pallas_call(functools.partial(backward_kernel, blocks, heads), out_sha...  38.9 us
    pallas_call x1, Pallas kernels, head_layer(): pl.pallas_call(functools.partial(head_kernel, n), out_shape=(jax.ShapeDty...  30.8 us
    pallas_call x1, Pallas kernels, attention_forward(): pl.pallas_call(functools.partial(forward_kernel, blocks, heads), out_shap...  20.3 us
  transfers between devices with their start and end apart: 2, of which 1 were waited for; matrix products, arithmetic and copies ran while one was open for 3% of the time, Pallas kernels for 38%

profile of v3, /device:TPU:0, one launch (start us, length us, event | category | flops | bytes accessed | tf_op | source)
XLA Modules:
  0.0 463.4 jit_solution(14966872277613374638)
XLA Ops:
  7.2 0.0 reduce-scatter.2.cloned.1.call-start
  7.2 1.4 pad_maximum_fusion
  8.6 30.8 %head_layer_0.1 = (bf16[8,512,288]{2,1,0:T(8,128)(2,1)}, bf16[512,768]{1,0:T(8,128)(2,1)}, f32[512,768]{1,0:T(8,128)}, f32[512,256]{1,0:T(8,128)}, f32[512,128]{...) custom-call(s32[2,8]{1,0:T(2,128)} %bitcast.28, s32[4]{0:T(128)} %lengths.5, ...), custom_call_target="tpu_custom_call" | custom-call | flops 2768240640 | bytes 25165824 | tf_op jit(solution)/shard_map/head_layer_0/pallas_call | solution.py:1643
  39.4 20.3 %attention_forward.1 = (f32[512,640]{1,0:T(8,128)}, bf16[512,640]{1,0:T(8,128)(2,1)}, f32[2,16,256]{2,1,0:T(8,128)}) custom-call(s32[2,8]{1,0:T(2,128)} %bitcast.29, s32[4]{0:T(128)} %lengths.5, bf16[2,10,256,256]{3,2,1,0:T(8,128)(2,1)} %get-tuple-element.55.qx, bf16[4096,288]{1,0:T(8,128)(2,1)} %bitcast.31, bf16[256,1280]{1,0:T(8,128)(2,1)} %wkvb.3), custom_call_target="tpu_custom_call" | custom-call | flops 10737418240 | bytes 16777216 | tf_op jit(solution)/shard_map/attention_forward/pallas_call | solution.py:208
  59.7 97.4 %middle_layer_5.1 = (bf16[32,16,2560]{2,1,0:T(8,128)(2,1)}, bf16[512,2560]{1,0:T(8,128)(2,1)}, bf16[512,2560]{1,0:T(8,128)(2,1)}, bf16[512,1600]{1,0:T(8,128)(2,...) custom-call(bf16[512,640]{1,0:T(8,128)(2,1)} %get-tuple-element.60.o, ...), custom_call_target="tpu_custom_call" | custom-call | flops 26843545600 | bytes 67108864 | tf_op jit(solution)/shard_map/middle_layer_5/pallas_call | solution.py:1405
  157.1 96.2 %gate_up_grads_1.1 = (bf16[320,1600]{1,0:T(8,128)(2,1)}, bf16[320,1600]{1,0:T(8,128)(2,1)}, bf16[512,2560]{1,0:T(8,128)(2,1)}, bf16[512,640]{1,0:T(8,128)(2,1)}, f32[1,2560]{1,0:T(1,128)}) custom-call(bf16[512,2560]{1,0:T(8,128)(2,1)} %get-tuple-element.61.normed, bf16[512,1600]{1,0:T(8,128)(2,1)} %get-tuple-element.62.d_gate, ...), custom_call_target="tpu_custom_call" | custom-call | flops 10066329600 | bytes 29360128 | tf_op jit(solution)/shard_map/gate_up_grads_1/pallas_call | solution.py:884
  253.2 0.0 reduce-scatter.2.cloned.1.call-update
  253.3 0.2 all-gather.2.cloned.1.call-start
  253.5 38.9 %attention_backward.1 = (bf16[512,960]{1,0:T(8,128)(2,1)}, bf16[4096,288]{1,0:T(8,128)(2,1)}, bf16[256,1280]{1,0:T(8,128)(2,1)}) custom-call(s32[2,8]{1,0:T(2,128)} %bitcast.30, s32[4]{0:T(128)} %lengths.5, bf16[2,10,256,256]{3,2,1,0:T(8,128)(2,1)} %get-tuple-element.55.qx, bf16[2,10,96,256]{3,2,1,0:T(8,128)(2,1)} %get-tuple-element.56.qt, ...), custom_call_target="tpu_custom_call" | custom-call | flops 21474836480 | bytes 25165824 | tf_op jit(solution)/shard_map/attention_backward/pallas_call | solution.py:403
  292.4 99.0 %up_tail_2.1 = (bf16[8,64,768]{2,1,0:T(8,128)(2,1)}, bf16[8,64,288]{2,1,0:T(8,128)(2,1)}, bf16[320,1600]{1,0:T(8,128)(2,1)}, bf16[320,640]{1,0:T(8,128)(2,1)}, b...) custom-call(bf16[4096,288]{1,0:T(8,128)(2,1)} %get-tuple-element.71.d_lat, bf16[512,960]{1,0:T(8,128)(2,1)} %get-tuple-element.72.d_query, ...), custom_call_target="tpu_custom_call" | custom-call | flops 7381975040 | bytes 33554432 | tf_op jit(solution)/shard_map/up_tail_2/pallas_call | solution.py:1023
  391.4 0.0 copy-start.5
  391.4 0.0 copy-start.6
  391.4 0.0 reduce-scatter.2.cloned.1.call-done
  391.5 2.8 add_convert_fusion
  394.2 0.0 all-gather.2.cloned.1.call-update
  394.3 0.8 convert_element_type.43
  395.1 0.7 convert_element_type.44
  395.7 0.9 convert_element_type.45
  396.7 1.5 convert_element_type.46
  398.2 1.5 convert_element_type.47
  399.6 1.5 convert_element_type.48
  401.1 39.3 %down_tail_3.1 = (f32[512,2560]{1,0:T(8,128)}, bf16[320,768]{1,0:T(8,128)(2,1)}, bf16[320,288]{1,0:T(8,128)(2,1)}, bf16[32,128]{1,0:T(8,128)(2,1)}) custom-call(bf16[512,768]{1,0:T(8,128)(2,1)} %bitcast.34, bf16[512,288]{1,0:T(8,128)(2,1)} %bitcast.35, f32[512,768]{1,0:T(8,128)} %get-tuple-element.83.q_pre, f32[512,256]{1,0:T(8,128)} %get-tuple-element.84.lat_raw, ...), custom_call_target="tpu_custom_call" | custom-call | flops 5536481280 | bytes 41943040 | tf_op jit(solution)/shard_map/down_tail_3/pallas_call | solution.py:1186
  440.5 0.7 bitcast_convert_fusion
  441.2 0.5 slice.17
  441.7 0.6 slice.18
  442.2 2.0 convert_element_type.41
  444.3 1.9 copy.31
  446.1 0.7 fusion
  446.8 3.1 all-gather.2.cloned.1.call-done
  449.9 3.6 copy.34
  453.4 0.4 copy-done
  453.8 2.4 copy.35
  (11 shorter events, 0.0 us)
Async XLA Ops:
  7.2 384.3 %reduce-scatter.2.cloned.1.call-start = ((), (), s32[]{:S(2)}) async-start(), calls=%async_computation.1 | async-start | bytes 3276800 | tf_op jit(solution)/shard_map/reduce_scatter | solution.py:1737
  253.3 196.6 %all-gather.2.cloned.1.call-start = ((), (), s32[]{:S(2)}) async-start(), calls=%async_computation.2 | async-start | bytes 3276800 | tf_op jit(solution)/shard_map/all_gather | solution.py:1753
  391.4 2.9 copy-start.5
  391.4 3.7 copy-start.6
  391.4 4.3 copy-start.4
  391.4 5.3 %copy-start.2 = (bf16[320,1600]{1,0:T(8,128)(2,1)S(1)}, bf16[320,1600]{1,0:T(8,128)(2,1)}, u32[]{:S(2)}) copy-start(bf16[320,1600]{1,0:T(8,128)(2,1)} %get-tuple-element.92) | copy-start | bytes 3072004
  394.3 3.9 copy-start.1
  396.7 2.9 copy-start.3
  449.9 3.9 copy-start
Sparse Core Ops, SparseCore 0:
  253.4 54.3 reduce-scatter.1
  394.4 55.4 all-gather.1

commit v4 on v3

--- a/solution.py
+++ b/solution.py
@@ -1270,11 +1270,11 @@
         for k, (source, target) in enumerate(
             (
                 (w_out, wo),
+                (cot_in, cot),
+                (w_down, wd),
                 (tokens_in, tokens),
-                (cot_in, cot),
                 (w_gate, wg),
                 (w_up, wu),
-                (w_down, wd),
             )
         )
     ]
@@ -1315,18 +1315,24 @@
             middle = tokens[rows, :].astype(jnp.float32) + RESIDUAL_SCALE * sums.astype(jnp.float32)
             h_out[rows, :] = (middle * norm_scale(middle) * gain[:, width : 2 * width]).astype(jnp.bfloat16)
 
+    def feed_first(b, i):
+        rows = pl.ds(pl.multiple_of(b * BLOCK, BLOCK), BLOCK)
+        first, last = cuts[i], cuts[i + 1]
+        if i == 0:
+            df_out[rows, :] = (RESIDUAL_SCALE * cot[rows, :].astype(jnp.float32)).astype(
+                jnp.bfloat16
+            )
+        du_out[rows, first:last] = dot_nt(df_out[rows, :], wd[first:last, :]).astype(jnp.bfloat16)
+
     def feed(b, i):
         rows = pl.ds(pl.multiple_of(b * BLOCK, BLOCK), BLOCK)
         first, last = cuts[i], cuts[i + 1]
         if i == 0:
             normalize(b, 0)
             normalize(b, 1)
-            df_out[rows, :] = (RESIDUAL_SCALE * cot[rows, :].astype(jnp.float32)).astype(
-                jnp.bfloat16
-            )
         gate = dot_nt(h_out[rows, :], wg[first:last, :])
         upper = dot_nt(h_out[rows, :], wu[first:last, :])
-        d_act = dot_nt(df_out[rows, :], wd[first:last, :])
+        d_act = du_out[rows, first:last].astype(jnp.float32)
         sig = jax.nn.sigmoid(gate)
         silu = gate * sig
         act_out[rows, first:last] = (silu * upper).astype(jnp.bfloat16)
@@ -1354,13 +1360,15 @@
 
     loads[0].wait()
     lax.fori_loop(0, blocks, project, 0)
+    for load in loads[1:3]:
+        load.wait()
 
     def outer(o, carry):
         b = o - block_lag
 
         @pl.when(b == 0)
         def _():
-            for load in loads[1:]:
+            for load in loads[3:]:
                 load.wait()
 
         share = per_block // 8
@@ -1371,6 +1379,10 @@
                 def _(at=(2 * i + step) * share):
                     for k in range(share):
                         line.duty(o * per_block + at + k)
+
+                @pl.when(2 * o < blocks)
+                def _(slot=2 * i + step):
+                    feed_first(2 * o + slot // 4, slot % 4)
 
                 @pl.when(b >= 0)
                 def _(i=i, work=work):

time: 470 us -> 470 us (level)
    pallas_call x1, Pallas kernels: 38.9 us -> 49.8 us  [attention_backward(): pl.pallas_call(functools.partial(backward_kernel, blocks, heads), out_sha...]
    pallas_call x1, Pallas kernels: 99 us -> 89.7 us  [up_tail(): pl.pallas_call(functools.partial(up_tail_kernel, n, tp, plans), out_shape...]
    pallas_call x1, Pallas kernels: 20.3 us -> 26.7 us  [attention_forward(): pl.pallas_call(functools.partial(forward_kernel, blocks, heads), out_shap...]
where the time goes in v4:
time: 470 us; the launch traced here: 466 us
  Pallas kernels  424 us (90%)
  between operations  14.4 us (3%)
  other arithmetic  13.7 us (3%)
  local copies, waits for them, and re-layouts  9.91 us (2%)
    pallas_call x1, Pallas kernels, middle_layer(): pl.pallas_call(functools.partial(middle_kernel, n, LAG), out_shape=(jax.S...  94.5 us
    pallas_call x1, Pallas kernels, gate_up_grads(): pl.pallas_call(functools.partial(gate_up_kernel, n, tp, plans), out_shape...  92.4 us
    pallas_call x1, Pallas kernels, up_tail(): pl.pallas_call(functools.partial(up_tail_kernel, n, tp, plans), out_shape...  89.7 us
    pallas_call x1, Pallas kernels, attention_backward(): pl.pallas_call(functools.partial(backward_kernel, blocks, heads), out_sha...  49.8 us
    pallas_call x1, Pallas kernels, down_tail(): pl.pallas_call(functools.partial(down_tail_kernel, n, plans), out_shape=(...  39.7 us
    pallas_call x1, Pallas kernels, head_layer(): pl.pallas_call(functools.partial(head_kernel, n), out_shape=(jax.ShapeDty...  30.8 us
    pallas_call x1, Pallas kernels, attention_forward(): pl.pallas_call(functools.partial(forward_kernel, blocks, heads), out_shap...  26.7 us
  transfers between devices with their start and end apart: 2, of which 1 were waited for; matrix products, arithmetic and copies ran while one was open for 3% of the time, Pallas kernels for 38%

profile of v4, /device:TPU:0, one launch (start us, length us, event | category | flops | bytes accessed | tf_op | source)
XLA Modules:
  0.0 466.1 jit_solution(7483514471957055900)
XLA Ops:
  7.2 0.0 reduce-scatter.2.cloned.1.call-start
  7.2 1.4 pad_maximum_fusion
  8.6 30.8 %head_layer_0.1 = (bf16[8,512,288]{2,1,0:T(8,128)(2,1)}, bf16[512,768]{1,0:T(8,128)(2,1)}, f32[512,768]{1,0:T(8,128)}, f32[512,256]{1,0:T(8,128)}, f32[512,128]{...) custom-call(s32[2,8]{1,0:T(2,128)} %bitcast.28, s32[4]{0:T(128)} %lengths.5, ...), custom_call_target="tpu_custom_call" | custom-call | flops 2768240640 | bytes 25165824 | tf_op jit(solution)/shard_map/head_layer_0/pallas_call | solution.py:1655
  39.4 26.7 %attention_forward.1 = (f32[512,640]{1,0:T(8,128)}, bf16[512,640]{1,0:T(8,128)(2,1)}, f32[2,16,256]{2,1,0:T(8,128)}) custom-call(s32[2,8]{1,0:T(2,128)} %bitcast.29, s32[4]{0:T(128)} %lengths.5, bf16[2,10,256,256]{3,2,1,0:T(8,128)(2,1)} %get-tuple-element.55.qx, bf16[4096,288]{1,0:T(8,128)(2,1)} %bitcast.31, bf16[256,1280]{1,0:T(8,128)(2,1)} %wkvb.3), custom_call_target="tpu_custom_call" | custom-call | flops 10737418240 | bytes 16777216 | tf_op jit(solution)/shard_map/attention_forward/pallas_call | solution.py:208
  66.1 94.5 %middle_layer_5.1 = (bf16[32,16,2560]{2,1,0:T(8,128)(2,1)}, bf16[512,2560]{1,0:T(8,128)(2,1)}, bf16[512,2560]{1,0:T(8,128)(2,1)}, bf16[512,1600]{1,0:T(8,128)(2,...) custom-call(bf16[512,640]{1,0:T(8,128)(2,1)} %get-tuple-element.60.o, ...), custom_call_target="tpu_custom_call" | custom-call | flops 26843545600 | bytes 67108864 | tf_op jit(solution)/shard_map/middle_layer_5/pallas_call | solution.py:1417
  160.6 92.4 %gate_up_grads_1.1 = (bf16[320,1600]{1,0:T(8,128)(2,1)}, bf16[320,1600]{1,0:T(8,128)(2,1)}, bf16[512,2560]{1,0:T(8,128)(2,1)}, bf16[512,640]{1,0:T(8,128)(2,1)}, f32[1,2560]{1,0:T(1,128)}) custom-call(bf16[512,2560]{1,0:T(8,128)(2,1)} %get-tuple-element.61.normed, bf16[512,1600]{1,0:T(8,128)(2,1)} %get-tuple-element.62.d_gate, ...), custom_call_target="tpu_custom_call" | custom-call | flops 10066329600 | bytes 29360128 | tf_op jit(solution)/shard_map/gate_up_grads_1/pallas_call | solution.py:884
  253.0 0.0 reduce-scatter.2.cloned.1.call-update
  253.1 0.4 all-gather.2.cloned.1.call-start
  253.5 49.8 %attention_backward.1 = (bf16[512,960]{1,0:T(8,128)(2,1)}, bf16[4096,288]{1,0:T(8,128)(2,1)}, bf16[256,1280]{1,0:T(8,128)(2,1)}) custom-call(s32[2,8]{1,0:T(2,128)} %bitcast.30, s32[4]{0:T(128)} %lengths.5, bf16[2,10,256,256]{3,2,1,0:T(8,128)(2,1)} %get-tuple-element.55.qx, bf16[2,10,96,256]{3,2,1,0:T(8,128)(2,1)} %get-tuple-element.56.qt, ...), custom_call_target="tpu_custom_call" | custom-call | flops 21474836480 | bytes 25165824 | tf_op jit(solution)/shard_map/attention_backward/pallas_call | solution.py:403
  303.3 89.7 %up_tail_2.1 = (bf16[8,64,768]{2,1,0:T(8,128)(2,1)}, bf16[8,64,288]{2,1,0:T(8,128)(2,1)}, bf16[320,1600]{1,0:T(8,128)(2,1)}, bf16[320,640]{1,0:T(8,128)(2,1)}, b...) custom-call(bf16[4096,288]{1,0:T(8,128)(2,1)} %get-tuple-element.71.d_lat, bf16[512,960]{1,0:T(8,128)(2,1)} %get-tuple-element.72.d_query, ...), custom_call_target="tpu_custom_call" | custom-call | flops 7381975040 | bytes 33554432 | tf_op jit(solution)/shard_map/up_tail_2/pallas_call | solution.py:1023
  393.0 0.0 copy-start.5
  393.0 0.0 copy-start.6
  393.1 0.0 reduce-scatter.2.cloned.1.call-done
  393.1 2.8 add_convert_fusion
  395.8 0.0 all-gather.2.cloned.1.call-update
  395.9 0.8 convert_element_type.43
  396.7 0.7 convert_element_type.44
  397.4 0.9 convert_element_type.45
  398.3 1.5 convert_element_type.46
  399.8 1.5 convert_element_type.47
  401.3 1.5 convert_element_type.48
  402.7 39.7 %down_tail_3.1 = (f32[512,2560]{1,0:T(8,128)}, bf16[320,768]{1,0:T(8,128)(2,1)}, bf16[320,288]{1,0:T(8,128)(2,1)}, bf16[32,128]{1,0:T(8,128)(2,1)}) custom-call(bf16[512,768]{1,0:T(8,128)(2,1)} %bitcast.34, bf16[512,288]{1,0:T(8,128)(2,1)} %bitcast.35, f32[512,768]{1,0:T(8,128)} %get-tuple-element.83.q_pre, f32[512,256]{1,0:T(8,128)} %get-tuple-element.84.lat_raw, ...), custom_call_target="tpu_custom_call" | custom-call | flops 5536481280 | bytes 41943040 | tf_op jit(solution)/shard_map/down_tail_3/pallas_call | solution.py:1186
  442.4 0.7 bitcast_convert_fusion
  443.1 0.5 slice.17
  443.6 0.6 slice.18
  444.2 2.0 convert_element_type.41
  446.2 1.9 copy.31
  448.1 0.7 fusion
  448.7 4.0 all-gather.2.cloned.1.call-done
  452.7 3.6 copy.34
  456.3 0.4 copy-done
  456.7 2.4 copy.35
  (11 shorter events, 0.0 us)
Async XLA Ops:
  7.2 385.9 %reduce-scatter.2.cloned.1.call-start = ((), (), s32[]{:S(2)}) async-start(), calls=%async_computation.1 | async-start | bytes 3276800 | tf_op jit(solution)/shard_map/reduce_scatter | solution.py:1749
  253.1 199.7 %all-gather.2.cloned.1.call-start = ((), (), s32[]{:S(2)}) async-start(), calls=%async_computation.2 | async-start | bytes 3276800 | tf_op jit(solution)/shard_map/all_gather | solution.py:1765
  393.0 2.9 copy-start.5
  393.0 3.7 copy-start.6
  393.0 4.3 copy-start.4
  393.0 5.3 %copy-start.2 = (bf16[320,1600]{1,0:T(8,128)(2,1)S(1)}, bf16[320,1600]{1,0:T(8,128)(2,1)}, u32[]{:S(2)}) copy-start(bf16[320,1600]{1,0:T(8,128)(2,1)} %get-tuple-element.92) | copy-start | bytes 3072004
  395.9 3.9 copy-start.1
  398.3 2.9 copy-start.3
  452.7 3.9 copy-start
Sparse Core Ops, SparseCore 0:
  253.2 53.7 reduce-scatter.1
  396.0 56.6 all-gather.1
